TPU v7x, 512 devices: a whole 4x8x8 slice. The times are simulated.
512 devices in a mesh: dp: 16 (over y, core), label: 32 (over z, x).
Axes of the slice: x: 4, y: 8, z: 8, core: 2. Of those that a mesh axis runs over, the one named last changes fastest.
Arguments:
- feats: bfloat16 [8192, 1024], P('dp'), may hold values from -2 to 2
- weights: bfloat16 [2048, 256, 1024], P(('dp', 'label')), may hold values from -5 to 5
- shortlist: int32 [64, 256], replicated, may hold values from 0 to 2047, as said below
- slot_of: int32 [2048], replicated, may hold values from 0 to 2047, as said below
- positives: int32 [8192, 8], P('dp'), may hold values from 0 to 524287, as said below
Outputs:
- loss: float32 [8192], P('dp')
- grad_feats: bfloat16 [8192, 1024], P('dp', 'label')
Inputs may be any that keep to these rules, and one draw needn't show every extreme that they name: `slot_of`: A permutation of the cluster ids: the slot of each cluster. For each index d of dp, its blocks d * 4 to d * 4 + 3: the first 2 of them together shortlist one cluster stored on each device (the device of slot s being s // 4 in the order of the weights' placement), each once, and the last 2 shortlist the same clusters, each once; so every such cluster is shortlisted by exactly two blocks of d. `positives`: an instance's 8 labels are different, and each lies in a cluster that the instance's block shortlists.
All inputs are finite; a program needn't handle non-finite values.
Results may differ from a plain program's by a relative error of at most 0.0034.
Values may be sent and summed in bfloat16 or wider, within the bound.
A program may use at most 64 MiB of HBM per device.

v0:
```python
import jax
import jax.numpy as jnp
from jax import lax
from jax.sharding import PartitionSpec as P

BLK = 128


neg_fill = -1e30


def slot_summary(logits, target):
    highest = jnp.max(logits, axis=1)
    total = jnp.sum(jnp.exp(logits - highest[:, None]), axis=1)
    return (highest, total, jnp.sum(target * logits, axis=1))


def shards(feats, weights, shortlist, slot_of, positives):
    dp_count = lax.axis_size("dp")
    lab_count = lax.axis_size("label")
    dp_index = lax.axis_index("dp")
    lab_index = lax.axis_index("label")
    my_device = dp_index * lab_count + lab_index
    stored_count, cluster_size, width_full = weights.shape
    inst_count = feats.shape[0]
    pos_count = positives.shape[1]
    block_count = inst_count // BLK
    half_count = block_count // 2
    short_count = shortlist.shape[1]
    all_lists = shortlist.reshape(dp_count, block_count, short_count)
    first_half = all_lists[:, :half_count, :].reshape(dp_count, half_count * short_count)
    first_slots = jnp.take(slot_of, first_half)
    first_dev = first_slots // stored_count
    picked = jnp.sum(jnp.where(first_dev == my_device, first_slots % stored_count, 0), axis=1)
    outgoing = jnp.take(weights, picked, axis=0)
    arrived = lax.all_to_all(outgoing, "dp", split_axis=0, concat_axis=0, tiled=True)
    my_lists = lax.dynamic_index_in_dim(all_lists, dp_index, 0, keepdims=False)
    my_first = lax.dynamic_index_in_dim(first_half, dp_index, 0, keepdims=False)
    my_dev = lax.dynamic_index_in_dim(first_dev, dp_index, 0, keepdims=False)
    source_dev = jnp.arange(dp_count, dtype=jnp.int32) * lab_count + lab_index
    matched = my_dev[None, :] == source_dev[:, None]
    slot_cluster = jnp.sum(jnp.where(matched, my_first[None, :], 0), axis=1)
    member = jnp.any(my_lists[None, :, :] == slot_cluster[:, None, None], axis=2)
    block_ids = jnp.arange(block_count, dtype=jnp.int32)
    low_block = jnp.sum(
        jnp.where(member & (block_ids < half_count)[None, :], block_ids[None, :], 0), axis=1
    )
    high_block = jnp.sum(
        jnp.where(member & (block_ids >= half_count)[None, :], block_ids[None, :], 0), axis=1
    )
    pair_table = jnp.stack([low_block, high_block], axis=1)
    hot_mask = (pair_table[:, :, None] == block_ids[None, None, :])[:, :, :, None]
    feat_blocks = feats.reshape(block_count, BLK, width_full)
    pos_blocks = positives.reshape(block_count, BLK, pos_count)
    offsets = jnp.arange(cluster_size, dtype=jnp.int32)

    def slot_logits(rows_in, pair_ids):
        pair_rows = jnp.take(feat_blocks, pair_ids, axis=0).reshape(2 * BLK, width_full)
        return jnp.einsum("id,od->io", pair_rows, rows_in, preferred_element_type=jnp.float32)

    def target_of(pair_ids, cluster):
        pos_pair = jnp.take(pos_blocks, pair_ids, axis=0).reshape(2 * BLK, pos_count)
        in_cluster = pos_pair // cluster_size == cluster
        at_offset = (pos_pair % cluster_size)[:, :, None] == offsets[None, None, :]
        return jnp.sum((in_cluster[:, :, None] & at_offset).astype(jnp.float32), axis=1)

    def first_pass(slot_items):
        rows_in, pair_ids, cluster = slot_items
        logits = slot_logits(rows_in, pair_ids)
        return (logits,) + slot_summary(logits, target_of(pair_ids, cluster))

    kept, slot_max, slot_total, slot_pos = lax.map(first_pass, (arrived, pair_table, slot_cluster))
    max_wide = slot_max.reshape(dp_count, 2, 1, BLK)
    total_wide = slot_total.reshape(dp_count, 2, 1, BLK)
    pos_wide = slot_pos.reshape(dp_count, 2, 1, BLK)
    local_max = jnp.max(jnp.where(hot_mask, max_wide, neg_fill), axis=(0, 1))
    pos_local = jnp.sum(jnp.where(hot_mask, pos_wide, 0.0), axis=(0, 1)).reshape(-1)
    highest = lax.pmax(local_max.reshape(-1), "label")
    scaled = total_wide * jnp.exp(max_wide - highest.reshape(block_count, BLK)[None, None, :, :])
    exp_local = jnp.sum(jnp.where(hot_mask, scaled, 0.0), axis=(0, 1)).reshape(-1)
    totals, pos_total = lax.psum((exp_local, pos_local), "label")
    log_sum = highest + jnp.log(totals)
    loss_rows = log_sum - pos_total / pos_count
    lse_blocks = log_sum.reshape(block_count, BLK)

    def grad_step(running, rows_in, pair_ids, cluster, logits):
        lse_pair = jnp.take(lse_blocks, pair_ids, axis=0).reshape(2 * BLK)
        dlogit = (
            jnp.exp(logits - lse_pair[:, None]) - target_of(pair_ids, cluster) / pos_count
        ).astype(jnp.bfloat16)
        term_grad = jnp.dot(dlogit, rows_in, preferred_element_type=jnp.float32).reshape(
            2, BLK, width_full
        )
        return running.at[pair_ids].add(term_grad)

    start = jnp.zeros((block_count, BLK, width_full), jnp.float32)

    def keep_step(running, slot_items):
        rows_in, pair_ids, cluster, logits = slot_items
        return (grad_step(running, rows_in, pair_ids, cluster, logits), None)

    running, unused = lax.scan(keep_step, start, (arrived, pair_table, slot_cluster, kept))
    partial_grad = running.reshape(inst_count, width_full)
    grads = lax.psum_scatter(partial_grad, "label", scatter_dimension=1, tiled=True).astype(
        jnp.bfloat16
    )
    return (loss_rows, grads)


def solution(mesh):
    in_specs = (P("dp", None), P(("dp", "label"), None, None), P(), P(), P("dp", None))
    out_specs = (P("dp"), P("dp", "label"))
    return jax.shard_map(shards, mesh=mesh, in_specs=in_specs, out_specs=out_specs, check_vma=False)
```

profile of v0, /device:TPU:6, one launch (start us, length us, event | category | flops | bytes accessed | tf_op | source)
XLA Modules:
  0.0 975.7 jit_solution(8376693920610643155)
XLA Ops:
  8.3 45.5 %gather_fusion.4 = s32[8192]{0:T(1024)S(1)} fusion(s32[2048]{0:T(1024)S(1)} %copy-done.1, s32[8192]{0:T(1024)S(1)} %broadcast_clamp_fusion), kind=kCustom, calls=%fused_computation.4 | custom fusion | bytes 98304 | tf_op jit(solution)/shard_map/jit(_take)/gather | solution.py:32
  54.4 4.6 gather_fusion.5
  59.0 7.5 broadcast_select_fusion.1
  66.5 7.4 all-to-all-start
  74.7 183.4 %all-to-all-done = bf16[16,256,1024]{2,1,0:T(8,128)(2,1)} async-done(((bf16[16,256,1024]{2,1,0:T(8,128)(2,1)}), bf16[16,256,1024]{2,1,0:T(8,128)(2,1)}, u32[]{:S(2)}, u32[]{:S(2)}) %all-to-all-start) | async-done | bytes 8388640 | tf_op jit(solution)/shard_map/all_to_all | solution.py:36
  258.1 153.3 %while.32 = (s32[]{:T(128)}, f32[16,256,256]{1,2,0:T(8,128)}, f32[16,256]{1,0:T(8,128)S(1)}, f32[16,256]{1,0:T(8,128)S(1)}, f32[16,256]{1,0:T(8,128)S(1)}, /*ind...) while((s32[]{:T(128)}, f32[16,256,256]{1,2,0:T(8,128)}, ...), condition=%wide.region_10.12_spmd.clone, body=%wide.region_5.11_spmd.clone.sunk | while | flops 136899856 | bytes 5336301 | solution.py:72
  260.3 2.9 convert_reduce_fusion.4
  269.9 2.9 convert_reduce_fusion.4
  279.5 2.9 convert_reduce_fusion.4
  289.1 2.9 convert_reduce_fusion.4
  298.6 2.9 convert_reduce_fusion.4
  308.2 2.9 convert_reduce_fusion.4
  317.8 2.9 convert_reduce_fusion.4
  327.4 2.9 convert_reduce_fusion.4
  337.0 2.9 convert_reduce_fusion.4
  346.6 2.9 convert_reduce_fusion.4
  356.2 2.9 convert_reduce_fusion.4
  365.7 2.9 convert_reduce_fusion.4
  375.3 2.9 convert_reduce_fusion.4
  384.9 2.9 convert_reduce_fusion.4
  394.5 2.9 convert_reduce_fusion.4
  404.1 2.9 convert_reduce_fusion.4
  411.6 72.8 %pmax.7 = f32[512]{0:T(512)S(1)} all-reduce(f32[512]{0:T(512)S(1)} %bitcast.193), channel_id=1, replica_groups=mesh['dp'=16,'label'=32] {'label'}, use_global_device_ids=true, to_apply=%region_12.14 | all-reduce | flops 512 | bytes 4096 | tf_op jit(solution)/shard_map/pmax | solution.py:78
  484.5 74.3 %all-reduce = (f32[512]{0:T(512)S(1)}, f32[512]{0:T(512)S(1)}) all-reduce(f32[512]{0:T(512)S(1)} %bitcast.190, f32[512]{0:T(512)S(1)} %bitcast.189), channel_id=1, replica_groups=mesh['dp'=16,'label'=32] {'label'}, use_global_device_ids=true, to_apply=%region_16.18 | all-reduce | flops 1024 | bytes 8192 | tf_op jit(solution)/shard_map/psum | solution.py:81
  561.0 185.9 %while.33 = (s32[]{:T(128)}, f32[4,128,1024]{2,1,0:T(8,128)}, s32[16,2]{1,0:T(8,128)S(1)}, f32[16,256,256]{1,2,0:T(8,128)}, f32[4,128]{1,0:T(4,128)S(1)}, /*inde...) while((s32[]{:T(128)}, f32[4,128,1024]{2,1,0:T(8,128)}, ...), condition=%wide.region_20.22_spmd.clone, body=%wide.region_17.21_spmd.clone.sunk | while | flops 136835344 | bytes 6903497 | solution.py:102
  563.4 2.9 convert_reduce_fusion.5
  569.5 3.1 scatter_fusion
  581.1 3.1 scatter_fusion
  586.6 2.9 convert_reduce_fusion.5
  592.7 3.1 scatter_fusion
  604.3 3.1 scatter_fusion
  616.0 3.1 scatter_fusion
  621.4 2.9 convert_reduce_fusion.5
  627.6 3.1 scatter_fusion
  639.2 3.1 scatter_fusion
  650.8 3.1 scatter_fusion
  662.4 3.1 scatter_fusion
  674.1 3.1 scatter_fusion
  679.5 2.9 convert_reduce_fusion.5
  685.7 3.1 scatter_fusion
  697.3 3.1 scatter_fusion
  708.9 3.1 scatter_fusion
  720.5 3.1 scatter_fusion
  726.0 2.9 convert_reduce_fusion.5
  732.2 3.1 scatter_fusion
  743.8 3.1 scatter_fusion
  746.9 2.9 copy.33
  749.9 217.6 %reduce-scatter.2.cloned.1.call-done = f32[512,32]{0,1:T(8,128)} async-done(((f32[512,1024]{0,1:T(8,128)}), f32[512,32]{0,1:T(8,128)}) %reduce-scatter.2.cloned.1.call-update) | async-done | bytes 65552 | tf_op jit(solution)/shard_map/reduce_scatter | solution.py:104
  (616 shorter events, 232.1 us)
Async XLA Ops:
  7.2 47.2 %copy-start = (bf16[4,256,1024]{2,1,0:T(8,128)(2,1)S(1)}, bf16[4,256,1024]{2,1,0:T(8,128)(2,1)}, u32[]{:S(2)}) copy-start(bf16[4,256,1024]{2,1,0:T(8,128)(2,1)} %param.12) | copy-start | bytes 6291460
  7.2 1.1 copy-start.1
  66.5 191.7 %copy-start.2 = (s32[512,8]{0,1:T(8,128)S(1)}, s32[512,8]{0,1:T(8,128)}, u32[]{:S(2)}) copy-start(s32[512,8]{0,1:T(8,128)} %param.15) | copy-start | bytes 49156
  66.5 191.7 %all-to-all-start = ((bf16[16,256,1024]{2,1,0:T(8,128)(2,1)}), bf16[16,256,1024]{2,1,0:T(8,128)(2,1)}, u32[]{:S(2)}, u32[]{:S(2)}) async-start(bf16[16,256,1024]{2,1,0:T(8,128)(2,1)} %broadcast_select_fusion.1), calls=%async_computation | async-start | bytes 16777216 | tf_op jit(solution)/shard_map/all_to_all | solution.py:36
  73.9 893.5 %reduce-scatter.2.cloned.1.call-start = ((), (), s32[]{:S(2)}) async-start(), calls=%async_computation.2 | async-start | bytes 2162688 | tf_op jit(solution)/shard_map/reduce_scatter | solution.py:104
Sparse Core Ops, SparseCore 0:
  750.0 217.4 reduce-scatter.1
where the time goes:
time: 980 us; the launch traced here: 976 us
  waiting for transfers between devices  401 us (41%)
  other arithmetic  186 us (19%)
  local copies, waits for them, and re-layouts  162 us (17%)
  blocking collectives  147 us (15%)
  matrix products  55.2 us (6%)
  between operations  14.3 us (1%)
    reduce_scatter x1, waiting for transfers between devices, shards(): lax.psum_scatter(partial_grad, 'label', scatter_dimension=1, tiled=True)  218 us
    all_to_all x1, waiting for transfers between devices, shards(): lax.all_to_all(outgoing, 'dp', split_axis=0, concat_axis=0, tiled=True)  183 us
    reduce_sum x32, other arithmetic, target_of(): jnp.sum((in_cluster[:, :, None] & at_offset).astype(jnp.float32), axis=1)  92.8 us
    psum x1, blocking collectives, shards(): totals, pos_total = lax.psum((exp_local, pos_local), 'label')  74.3 us
    pmax x1, blocking collectives, shards(): highest = lax.pmax(local_max.reshape(-1), 'label')  72.8 us
    scatter-add x16, other arithmetic, grad_step(): return running.at[pair_ids].add(term_grad)  49.5 us
    gather x3, local copies, waits for them, and re-layouts, shards(): first_slots = jnp.take(slot_of, first_half)  45.6 us
    dot_general x16, matrix products, slot_logits(): jnp.einsum('id,od->io', pair_rows, rows_in, preferred_element_type=jnp.fl...  33.6 us
  transfers between devices with their start and end apart: 2, of which 2 were waited for; matrix products, arithmetic and copies ran while one was open for 0% of the time, Pallas kernels for 0%

commit v1 on v0

v1 whole, which is shorter than its diff:
```python
import functools
import itertools

import jax
import jax.numpy as jnp
from jax import lax
from jax.experimental import pallas as pl
from jax.experimental.pallas import tpu as pltpu
from jax.sharding import PartitionSpec as P

BLK = 128
CORES = 2
X_CHIPS = 4
VMEM_LIMIT = 56 * 1024 * 1024
NEG_FILL = -1e30
MESH = pl.DeviceIdType.MESH


class Place:
    def __init__(self, y_count, z_count, x_count):
        dp, lab = lax.axis_index("dp"), lax.axis_index("label")
        self.dp, self.lab = dp, lab
        self.y, self.core = dp // CORES, dp % CORES
        self.z, self.x = lab // x_count, lab % x_count
        self.count = {"y": y_count, "z": z_count, "x": x_count}
        self.pos = {"y": self.y, "z": self.z, "x": self.x}

    def at(self, axis, offset):
        n = self.count[axis]
        return lax.rem(self.pos[axis] + (offset % n), n)

    def device(self, axis, offset):
        p = self.at(axis, offset)
        if axis == "y":
            return (p * CORES + self.core, self.lab)
        if axis == "z":
            return (self.dp, p * self.count["x"] + self.x)
        return (self.dp, self.z * self.count["x"] + p)

    def sibling(self):
        return (self.y * CORES + (1 - self.core), self.lab)


def greet(devices):
    barrier = pltpu.get_barrier_semaphore()
    for device in devices:
        pl.semaphore_signal(barrier, inc=1, device_id=device, device_id_type=MESH)
    pl.semaphore_wait(barrier, len(devices))


class Sender:
    def __init__(self, send_sem, recv_sem):
        self.send_sem, self.recv_sem = send_sem, recv_sem
        self.ids = itertools.count()
        self.sent = []

    def start(self, src, dst, device):
        i = next(self.ids)
        copy = pltpu.make_async_remote_copy(
            src_ref=src,
            dst_ref=dst,
            send_sem=self.send_sem.at[i],
            recv_sem=self.recv_sem.at[i],
            device_id=device,
            device_id_type=MESH,
        )
        copy.start()
        self.sent.append(copy)
        return copy

    def drain(self):
        for copy in self.sent:
            copy.wait_send()


def reach(n, sign, half):
    return n // 2 if (sign > 0) == (half == 0) else n // 2 - 1


class Spread:
    def __init__(self, place, axis, half, source, target, sender, arrived=None):
        self.place, self.axis, self.half = place, axis, half
        self.source, self.target, self.sender = source, target, sender
        self.arrived = arrived
        self.step = 0
        self.copies = {}

    def advance(self):
        n = self.place.count[self.axis]
        k = self.step
        born = []
        for sign in (1, -1):
            limit = reach(n, sign, self.half)
            origin = self.place.at(self.axis, -sign * k)
            if 1 <= k <= limit:
                self.copies[sign, k].wait_recv()
                if self.arrived is not None:
                    born += self.arrived(origin)
            if k + 1 <= limit:
                src = self.source() if k == 0 else self.target(origin)
                self.copies[sign, k + 1] = self.sender.start(
                    src, self.target(origin), self.place.device(self.axis, sign)
                )
        self.step += 1
        return born, self.step > n // 2


def run_all(tasks):
    while tasks:
        left, born_now = [], []
        for task in tasks:
            born, done = task.advance()
            born_now += born
            if not done:
                left.append(task)
        tasks = left + born_now


def gather_kernel(sizes, feats, pos, rows, f_all, p_all, w_sib, local_sem, send_sem, recv_sem):
    y_count, z_count, x_count = sizes
    place = Place(*sizes)
    inst, width = feats.shape
    a_total, b_total = inst // 2, inst // 4
    a_part, b_part = a_total // x_count, b_total // z_count
    c_total = inst - a_total - b_total
    greet(
        [place.device(axis, offset) for axis in "yxz" for offset in (1, -1)] + [place.sibling()]
    )
    sender = Sender(send_sem, recv_sem)
    mine = place.y

    def piece(start, count):
        start = pl.multiple_of(start, 16)
        return (
            lambda: feats.at[pl.ds(start, count)],
            lambda origin: f_all.at[origin, pl.ds(start, count)],
        )

    tasks = []
    a_half = a_part // 2
    for half in (0, 1):
        source, target = piece(c_total + place.x * a_part + half * a_half, a_half)

        def a_arrived(origin, half=half, target=target):
            def moved(o, origin=origin, half=half):
                start = pl.multiple_of(c_total + o * a_part + half * a_half, 16)
                return f_all.at[origin, pl.ds(start, a_half)]

            return [Spread(place, "x", half, lambda: target(origin), moved, sender)]

        tasks.append(Spread(place, "y", half, source, target, sender, a_arrived))
    source, target = piece(c_total + a_total + place.z * b_part, b_part)
    order = itertools.count()

    def b_arrived(origin, target=target):
        def moved(o, origin=origin):
            start = pl.multiple_of(c_total + a_total + o * b_part, 16)
            return f_all.at[origin, pl.ds(start, b_part)]

        return [Spread(place, "z", next(order) % 2, lambda: target(origin), moved, sender)]

    tasks.append(Spread(place, "y", 0, source, target, sender, b_arrived))
    tasks.append(Spread(place, "y", 1, lambda: pos, lambda origin: p_all.at[origin], sender))
    for half in (0, 1):
        source, target = piece(half * (c_total // 2), c_total // 2)
        tasks.append(Spread(place, "y", half, source, target, sender))

    swap = sender.start(rows, w_sib, place.sibling())
    keep_f = pltpu.make_async_copy(feats, f_all.at[mine], local_sem.at[0])
    keep_p = pltpu.make_async_copy(pos, p_all.at[mine], local_sem.at[1])
    keep_f.start()
    keep_p.start()
    run_all(tasks)
    swap.wait_recv()
    keep_f.wait()
    keep_p.wait()
    sender.drain()


def gather(sizes, feats, pos, rows):
    y_count, z_count, x_count = sizes
    copies = 6 * (y_count - 1) + (y_count - 1) * (2 * (x_count - 1) + z_count - 1) + 1
    return pl.pallas_call(
        functools.partial(gather_kernel, sizes),
        out_shape=(
            jax.ShapeDtypeStruct((y_count,) + feats.shape, feats.dtype),
            jax.ShapeDtypeStruct((y_count,) + pos.shape, pos.dtype),
            jax.ShapeDtypeStruct(rows.shape, rows.dtype),
        ),
        in_specs=[pl.BlockSpec(memory_space=pl.ANY)] * 3,
        out_specs=[pl.BlockSpec(memory_space=pl.ANY)] * 3,
        scratch_shapes=[
            pltpu.SemaphoreType.DMA((2,)),
            pltpu.SemaphoreType.DMA((copies,)),
            pltpu.SemaphoreType.DMA((copies,)),
        ],
        compiler_params=pltpu.CompilerParams(
            collective_id=0, has_side_effects=True, vmem_limit_bytes=VMEM_LIMIT
        ),
    )(feats, pos, rows)


def target_of(pos_ref, cluster, shape):
    size = shape[0]
    label = cluster * size + lax.broadcasted_iota(jnp.int32, shape, 0)
    hit = pos_ref[0, 0:1, :] == label
    for p in range(1, pos_ref.shape[1]):
        hit = hit | (pos_ref[0, p : p + 1, :] == label)
    return hit


def logits_kernel(pick, cluster, f_ref, own_ref, sib_ref, mask_ref, pos_ref, kept_ref, stat_ref):
    d = pl.program_id(0)
    feats = f_ref[0]
    highs, sums, hits = [], [], []
    for s, rows_ref in enumerate((own_ref, sib_ref)):
        logits = lax.dot_general(
            rows_ref[0], feats, (((1,), (1,)), ((), ())), preferred_element_type=jnp.float32
        )
        kept_ref[0, s] = logits
        valid = jnp.where(mask_ref[0, s : s + 1, :] > 0, logits, NEG_FILL)
        high = jnp.max(valid, axis=0, keepdims=True)
        highs.append(high)
        sums.append(jnp.sum(jnp.exp(valid - high), axis=0, keepdims=True))
        hit = target_of(pos_ref, cluster[d, s], logits.shape)
        hits.append(jnp.sum(jnp.where(hit, logits, 0.0), axis=0, keepdims=True))
    high = jnp.maximum(highs[0], highs[1])
    total = sums[0] * jnp.exp(highs[0] - high) + sums[1] * jnp.exp(highs[1] - high)
    stat_ref[0] = jnp.zeros_like(stat_ref[0])
    stat_ref[0, 0:1, :] = high
    stat_ref[0, 1:2, :] = total
    stat_ref[0, 2:3, :] = hits[0] + hits[1]


def grads_kernel(pick, cluster, own_ref, sib_ref, mask_ref, pos_ref, kept_ref, lse_ref, gx_ref, gz_ref):
    d = pl.program_id(0)
    pos_count = pos_ref.shape[1]
    shares = None
    lse = lse_ref[0, 0:1, :]
    for s, rows_ref in enumerate((own_ref, sib_ref)):
        logits = kept_ref[0, s]
        prob = jnp.where(mask_ref[0, s : s + 1, :] > 0, jnp.exp(logits - lse), 0.0)
        hit = target_of(pos_ref, cluster[d, s], logits.shape)
        dlogit = (prob - jnp.where(hit, 1.0 / pos_count, 0.0)).astype(jnp.bfloat16)
        term = lax.dot_general(
            rows_ref[0], dlogit, (((0,), (0,)), ((), ())), preferred_element_type=jnp.float32
        )
        shares = term if shares is None else shares + term
    half = shares.shape[1] // 2
    gx_ref[0] = shares[:, :half].astype(jnp.bfloat16)
    gz_ref[0] = shares[:, half:].astype(jnp.bfloat16)


def block(shape):
    return pl.BlockSpec((1,) + shape, lambda d, pick, cluster: (d,) + (0,) * len(shape))


def picked(s, rows):
    return pl.BlockSpec((1,) + rows.shape[1:], lambda d, pick, cluster: (pick[d, s], 0, 0))


def first_pass(pick, cluster, f_all, own, sib, mask, pos):
    y_count, inst, width = f_all.shape
    size = own.shape[1]
    return pl.pallas_call(
        logits_kernel,
        grid_spec=pltpu.PrefetchScalarGridSpec(
            num_scalar_prefetch=2,
            grid=(y_count,),
            in_specs=[
                block((inst, width)),
                picked(0, own),
                picked(1, sib),
                block((2, inst)),
                block(pos.shape[1:]),
            ],
            out_specs=[block((2, size, inst)), block((8, inst))],
        ),
        out_shape=(
            jax.ShapeDtypeStruct((y_count, 2, size, inst), jnp.float32),
            jax.ShapeDtypeStruct((y_count, 8, inst), jnp.float32),
        ),
        compiler_params=pltpu.CompilerParams(vmem_limit_bytes=VMEM_LIMIT),
    )(pick, cluster, f_all, own, sib, mask, pos)


def second_pass(pick, cluster, own, sib, mask, pos, kept, lse):
    y_count, _, size, inst = kept.shape
    width = own.shape[2]
    half = jax.ShapeDtypeStruct((y_count, width, inst // 2), jnp.bfloat16)
    return pl.pallas_call(
        grads_kernel,
        grid_spec=pltpu.PrefetchScalarGridSpec(
            num_scalar_prefetch=2,
            grid=(y_count,),
            in_specs=[
                picked(0, own),
                picked(1, sib),
                block((2, inst)),
                block(pos.shape[1:]),
                block((2, size, inst)),
                block((8, inst)),
            ],
            out_specs=[block((width, inst // 2))] * 2,
        ),
        out_shape=(half, half),
        compiler_params=pltpu.CompilerParams(vmem_limit_bytes=VMEM_LIMIT),
    )(pick, cluster, own, sib, mask, pos, kept, lse)


def merge(parts):
    high = parts[0][0:1]
    for part in parts[1:]:
        high = jnp.maximum(high, part[0:1])
    total = sum(part[1:2] * jnp.exp(part[0:1] - high) for part in parts)
    hits = sum(part[2:3] for part in parts)
    return high, total, hits


def lse_kernel(sizes, pos_count, stats, lse_all, loss, held, slots_y, slots_x, slots_z, send_sem, recv_sem):
    y_count, z_count, x_count = sizes
    place = Place(*sizes)
    greet(
        [
            place.device(axis, offset)
            for axis, n in (("y", y_count), ("x", x_count), ("z", z_count))
            for offset in range(1, n)
        ]
    )
    sender = Sender(send_sem, recv_sem)

    def write(ref, values):
        for row, value in enumerate(values):
            ref[row : row + 1, :] = value

    copies = [
        sender.start(stats.at[place.at("y", o)], slots_y.at[o - 1], place.device("y", o))
        for o in range(1, y_count)
    ]
    for copy in copies:
        copy.wait_recv()
    write(held.at[0], merge([stats[place.y]] + [slots_y[o - 1] for o in range(1, y_count)]))
    for stage, (axis, slots) in enumerate((("x", slots_x), ("z", slots_z))):
        n = place.count[axis]
        copies = [
            sender.start(held.at[stage], slots.at[o - 1], place.device(axis, o)) for o in range(1, n)
        ]
        for copy in copies:
            copy.wait_recv()
        merged = merge([held[stage]] + [slots[o - 1] for o in range(1, n)])
        if stage == 0:
            write(held.at[1], merged)
    high, total, hits = merged
    lse = high + jnp.log(total)
    loss[...] = jnp.broadcast_to(lse - hits / pos_count, loss.shape)
    held[2] = jnp.broadcast_to(lse, held.shape[1:])
    lse_all[place.y] = held[2]
    copies = [
        sender.start(held.at[2], lse_all.at[place.y], place.device("y", o))
        for o in range(1, y_count)
    ]
    for copy in copies:
        copy.wait_recv()
    sender.drain()


def exchange_lse(sizes, pos_count, stats):
    y_count, z_count, x_count = sizes
    tile = stats.shape[1:]
    copies = 2 * (y_count - 1) + (x_count - 1) + (z_count - 1)
    return pl.pallas_call(
        functools.partial(lse_kernel, sizes, pos_count),
        out_shape=(
            jax.ShapeDtypeStruct(stats.shape, jnp.float32),
            jax.ShapeDtypeStruct(tile, jnp.float32),
        ),
        in_specs=[pl.BlockSpec(memory_space=pltpu.VMEM)],
        out_specs=[pl.BlockSpec(memory_space=pltpu.VMEM)] * 2,
        scratch_shapes=[
            pltpu.VMEM((3,) + tile, jnp.float32),
            pltpu.VMEM((y_count - 1,) + tile, jnp.float32),
            pltpu.VMEM((x_count - 1,) + tile, jnp.float32),
            pltpu.VMEM((z_count - 1,) + tile, jnp.float32),
            pltpu.SemaphoreType.DMA((copies,)),
            pltpu.SemaphoreType.DMA((copies,)),
        ],
        compiler_params=pltpu.CompilerParams(collective_id=1, has_side_effects=True),
    )(stats)


class Chain:
    def __init__(self, place, axis, sign, half, own, slots, sender):
        self.place, self.axis, self.sign = place, axis, sign
        self.length = reach(place.count[axis], sign, half)
        self.own, self.slots, self.sender = own, slots, sender
        self.step = 0
        self.copies = []

    def advance(self):
        k = self.step
        if k > 0:
            self.copies[-1].wait_recv()
        if k < self.length:
            ref = self.own(self.place.at(self.axis, self.sign * (self.length - k)))
            if k > 0:
                add_into(self.slots.at[k - 1], ref)
                ref = self.slots.at[k - 1]
            self.copies.append(
                self.sender.start(ref, self.slots.at[k], self.place.device(self.axis, self.sign))
            )
        self.step += 1
        return [], self.step > self.length


def add_into(total, term):
    def one(i, carry):
        value = total[i].astype(jnp.float32) + term[i].astype(jnp.float32)
        total[i] = value.astype(total.dtype)
        return carry

    lax.fori_loop(0, total.shape[0], one, 0)


def reduce_kernel(sizes, gx, gz, out, *scratch):
    y_count, z_count, x_count = sizes
    place = Place(*sizes)
    slots = dict(zip(SLOT_NAMES, scratch))
    x_sum, z_sum, y_sum = scratch[len(SLOT_NAMES) : len(SLOT_NAMES) + 3]
    send_sem, recv_sem = scratch[-2:]
    y_half = y_count // 2
    greet([place.device(axis, offset) for axis in "xzy" for offset in (1, -1)])
    sender = Sender(send_sem, recv_sem)

    def halves(half):
        return pl.ds(half * y_half, y_half)

    def chains(name, axis, own):
        return [
            Chain(place, axis, sign, half, functools.partial(own, half), slots[name, sign, half], sender)
            for half, sign in ((0, 1), (1, -1), (1, 1), (0, -1))
            if reach(place.count[axis], sign, half) > 0
        ]

    def landed(name, axis, half):
        n = place.count[axis]
        return [
            slots[name, sign, half].at[reach(n, sign, half) - 1]
            for sign in (1, -1)
            if reach(n, sign, half) > 0
        ]

    run_all(
        chains("z1", "z", lambda half, dest: gz.at[halves(half), dest])
        + chains("x1", "x", lambda half, dest: gx.at[halves(half), :, dest])
    )
    for half in (0, 1):
        for total, first, name, axis in (
            (x_sum, gx.at[:, :, place.x], "x1", "x"),
            (z_sum, gz.at[:, place.z], "z1", "z"),
        ):
            parts = landed(name, axis, half)

            def one(i, carry, total=total, first=first, parts=parts, half=half):
                value = first[half * y_half + i].astype(jnp.float32)
                for part in parts:
                    value = value + part[i].astype(jnp.float32)
                total[half * y_half + i] = value
                return carry

            lax.fori_loop(0, y_half, one, 0)
    run_all(
        chains("x2", "z", lambda half, dest: x_sum.at[halves(half), dest])
        + chains("z2", "x", lambda half, dest: z_sum.at[halves(half), dest])
    )
    for half in (0, 1):
        for lane, first, name, axis in (
            (0, x_sum.at[:, place.z], "x2", "z"),
            (1, z_sum.at[:, place.x], "z2", "x"),
        ):
            parts = landed(name, axis, half)

            def one(i, carry, lane=lane, first=first, parts=parts, half=half):
                value = first[half * y_half + i]
                for part in parts:
                    value = value + part[i]
                y_sum[lane, half * y_half + i] = value
                return carry

            lax.fori_loop(0, y_half, one, 0)
    run_all(chains("y3", "y", lambda half, dest: y_sum.at[half, pl.ds(dest, 1)]))
    for half in (0, 1):
        value = y_sum[half, place.y]
        for part in landed("y3", "y", half):
            value = value + part[0]
        out[half] = value
    sender.drain()


SLOT_NAMES = [
    (name, sign, half)
    for name in ("z1", "x1", "x2", "z2", "y3")
    for half in (0, 1)
    for sign in (1, -1)
]


def reduce_shares(sizes, gx, gz):
    y_count, z_count, x_count = sizes
    lanes = gx.shape[2]
    rows = gx.shape[1] // (z_count * x_count)
    gx = gx.reshape(y_count, z_count, x_count, rows, lanes)
    gz = gz.reshape(y_count, z_count, x_count, rows, lanes)
    y_half = y_count // 2
    pieces = {
        "z1": (z_count, (y_half, x_count, rows, lanes), jnp.bfloat16),
        "x1": (x_count, (y_half, z_count, rows, lanes), jnp.bfloat16),
        "x2": (z_count, (y_half, rows, lanes), jnp.float32),
        "z2": (x_count, (y_half, rows, lanes), jnp.float32),
        "y3": (y_count, (1, rows, lanes), jnp.float32),
    }
    scratch, copies = [], 0
    for name, sign, half in SLOT_NAMES:
        n, shape, dtype = pieces[name]
        steps = reach(n, sign, half)
        copies += steps
        scratch.append(pltpu.VMEM((max(steps, 1),) + shape, dtype))
    scratch += [
        pltpu.VMEM((y_count, z_count, rows, lanes), jnp.float32),
        pltpu.VMEM((y_count, x_count, rows, lanes), jnp.float32),
        pltpu.VMEM((2, y_count, rows, lanes), jnp.float32),
        pltpu.SemaphoreType.DMA((copies,)),
        pltpu.SemaphoreType.DMA((copies,)),
    ]

    return pl.pallas_call(
        functools.partial(reduce_kernel, sizes),
        out_shape=jax.ShapeDtypeStruct((2, rows, lanes), jnp.float32),
        in_specs=[pl.BlockSpec(memory_space=pltpu.VMEM)] * 2,
        out_specs=pl.BlockSpec(memory_space=pltpu.VMEM),
        scratch_shapes=scratch,
        compiler_params=pltpu.CompilerParams(
            collective_id=2, has_side_effects=True, vmem_limit_bytes=VMEM_LIMIT
        ),
    )(gx, gz)


def shards(x_count, feats, weights, shortlist, slot_of, positives):
    y_count = lax.axis_size("dp") // CORES
    lab_count = lax.axis_size("label")
    sizes = (y_count, lab_count // x_count, x_count)
    dp_index, lab_index = lax.axis_index("dp"), lax.axis_index("label")
    core = dp_index % CORES
    stored, size, width = weights.shape
    inst, pos_count = positives.shape
    block_count = inst // BLK
    half_blocks = block_count // 2
    pair = jnp.stack([dp_index, dp_index + 1 - 2 * core]) * lab_count + lab_index
    slots = (pair[:, None] * stored + jnp.arange(stored, dtype=jnp.int32)).reshape(-1)
    ids = jnp.arange(slot_of.shape[0], dtype=jnp.int32)
    clusters = jnp.sum(jnp.where(slots[:, None] == slot_of[None, :], ids[None, :], 0), axis=1)
    lists = shortlist.reshape(y_count, CORES, block_count, -1)
    lists = lax.dynamic_index_in_dim(lists, core, 1, keepdims=False)
    member = jnp.any(lists[:, :, None, :] == clusters[None, None, :, None], axis=3)
    member = member.reshape(y_count, block_count, CORES, stored).astype(jnp.int32)
    chosen = jnp.sum(member[:, :half_blocks], axis=1)
    pick = jnp.sum(chosen * jnp.arange(stored, dtype=jnp.int32), axis=2)
    cluster = jnp.sum(chosen * clusters.reshape(1, CORES, stored), axis=2)
    mask = jnp.sum(member, axis=3).astype(jnp.float32).transpose(0, 2, 1)
    mask = jnp.broadcast_to(mask[..., None], mask.shape + (BLK,)).reshape(y_count, CORES, inst)

    f_all, p_all, sib = gather(sizes, feats, positives.T, weights)
    kept, stats = first_pass(pick, cluster, f_all, weights, sib, mask, p_all)
    lse, loss = exchange_lse(sizes, pos_count, stats)
    gx, gz = second_pass(pick, cluster, weights, sib, mask, p_all, kept, lse)
    grads = reduce_shares(sizes, gx, gz)
    grads = grads.transpose(0, 2, 1).reshape(inst, -1)
    return loss[0], grads.astype(jnp.bfloat16)


def solution(mesh, x_count=X_CHIPS):
    in_specs = (P("dp", None), P(("dp", "label"), None, None), P(), P(), P("dp", None))
    out_specs = (P("dp"), P("dp", "label"))
    return jax.shard_map(
        functools.partial(shards, x_count),
        mesh=mesh,
        in_specs=in_specs,
        out_specs=out_specs,
        check_vma=False,
    )
```

time: 980 us -> 231 us (0.24)
  waiting for transfers between devices: 401 us -> 0 us
  Pallas kernels: 0 us -> 219 us
  other arithmetic: 186 us -> 2.74 us
  local copies, waits for them, and re-layouts: 162 us -> 5.19 us
  blocking collectives: 147 us -> 0 us
  matrix products: 55.2 us -> 0 us
  between operations: 14.3 us -> 0.72 us
    pallas_call x0 -> x5, Pallas kernels: none -> 219 us  [the longest x1 83.5 us: gather(): pl.pallas_call(functools.partial(gather_kernel, sizes), out_shape=(jax.Sh...]
    reduce_scatter x1 -> x0, waiting for transfers between devices: 218 us -> none  [shards(): lax.psum_scatter(partial_grad, 'label', scatter_dimension=1, tiled=True)]
    all_to_all x1 -> x0, waiting for transfers between devices: 183 us -> none  [shards(): lax.all_to_all(outgoing, 'dp', split_axis=0, concat_axis=0, tiled=True)]
    gather x68 -> x0, local copies, waits for them, and re-layouts: 106 us -> none  [the longest x3 45.6 us: shards(): first_slots = jnp.take(slot_of, first_half)]
    reduce_sum x52 -> x4, other arithmetic: 94.9 us -> 1.02 us  [the longest x1 0.89 us: shards(): jnp.sum(jnp.where(slots[:, None] == slot_of[None, :], ids[None, :], 0), a...]
    psum x1 -> x0, blocking collectives: 74.3 us -> none  [shards(): totals, pos_total = lax.psum((exp_local, pos_local), 'label')]
    pmax x1 -> x0, blocking collectives: 72.8 us -> none  [shards(): highest = lax.pmax(local_max.reshape(-1), 'label')]
    dot_general x32 -> x0, matrix products: 55.2 us -> none  [the longest x16 33.6 us: slot_logits(): jnp.einsum('id,od->io', pair_rows, rows_in, preferred_element_type=jnp.fl...]
  transfers between devices with their start and end apart: 2 -> 0, of which waited for: 2 -> 0; matrix products, arithmetic and copies ran while one was open for 0% -> 0% of each run, Pallas kernels for 0% -> 0%
where the time goes in v1:
time: 231 us; the launch traced here: 228 us
  Pallas kernels  219 us (95%)
  local copies, waits for them, and re-layouts  5.19 us (2%)
  other arithmetic  2.74 us (1%)
    pallas_call x1, Pallas kernels, gather(): pl.pallas_call(functools.partial(gather_kernel, sizes), out_shape=(jax.Sh...  83.5 us
    pallas_call x1, Pallas kernels, reduce_shares(): pl.pallas_call(functools.partial(reduce_kernel, sizes), out_shape=jax.Sha...  77.6 us
    pallas_call x1, Pallas kernels, exchange_lse(): pl.pallas_call(functools.partial(lse_kernel, sizes, pos_count), out_shape...  25.6 us
    pallas_call x1, Pallas kernels, second_pass(): pl.pallas_call(grads_kernel, grid_spec=pltpu.PrefetchScalarGridSpec(num_s...  16.4 us
    pallas_call x1, Pallas kernels, first_pass(): pl.pallas_call(logits_kernel, grid_spec=pltpu.PrefetchScalarGridSpec(num_...  16.1 us

profile of v1, /device:TPU:6, one launch (start us, length us, event | category | flops | bytes accessed | tf_op | source)
XLA Modules:
  0.0 227.9 jit_solution(16173498887904179155)
XLA Ops:
  0.6 0.9 reshape.62
  1.5 0.1 fusion.1
  1.6 0.1 iota_add_fusion
  1.7 0.1 add.49
  1.8 0.9 select_reduce_fusion
  2.7 0.7 compare_reduce_fusion
  3.4 0.1 copy.24
  3.5 0.1 mul.41
  3.6 0.1 multiply_reduce_fusion
  3.6 0.7 copy.26.pick
  4.3 0.7 copy.27.cluster
  5.0 83.5 %shard_map.68 = (bf16[8,512,1024]{2,1,0:T(8,128)(2,1)}, s32[8,8,512]{2,1,0:T(8,128)}, bf16[4,256,1024]{2,1,0:T(8,128)(2,1)}) custom-call(bf16[512,1024]{1,0:T(8,128)(2,1)} %feats.1, s32[8,512]{1,0:T(8,128)} %bitcast.20, bf16[4,256,1024]{2,1,0:T(8,128)(2,1)} %own_ref.3), custom_call_target="tpu_custom_call" | custom-call | tf_op jit(solution)/shard_map/pallas_call | solution.py:183
  88.5 0.1 copy.25
  88.6 0.1 broadcast_in_dim.16
  88.7 0.7 reshape.63.mask_ref
  89.3 16.1 %shard_map.69 = (f32[8,2,256,512]{3,2,1,0:T(8,128)}, f32[8,8,512]{2,1,0:T(8,128)}) custom-call(s32[8,2]{1,0:T(8,128)} %copy.26.pick, s32[8,2]{1,0:T(8,128)} %copy.27.cluster, bf16[8,512,1024]{2,1,0:T(8,128)(2,1)} %get-tuple-element.11.f_ref, bf16[4,256,1024]{2,1,0:T(8,128)(2,1)} %own_ref.3, bf16[4,256,1024]{2,1,0:T(8,128)(2,1)} %get-tuple-element.12.sib_ref, ...), custom_call_target="tpu_custom_call" | custom-call | tf_op jit(solution)/shard_map/pallas_call | solution.py:265
  105.5 25.6 %shard_map.70 = (f32[8,8,512]{2,1,0:T(8,128)}, f32[8,512]{1,0:T(8,128)}) custom-call(f32[8,8,512]{2,1,0:T(8,128)} %get-tuple-element.14.stats), custom_call_target="tpu_custom_call" | custom-call | tf_op jit(solution)/shard_map/pallas_call | solution.py:371
  131.1 1.3 slice.7
  132.4 16.4 %shard_map.71 = (bf16[8,1024,256]{2,1,0:T(8,128)(2,1)}, bf16[8,1024,256]{2,1,0:T(8,128)(2,1)}) custom-call(s32[8,2]{1,0:T(8,128)} %copy.26.pick, s32[8,2]{1,0:T(8,128)} %copy.27.cluster, bf16[4,256,1024]{2,1,0:T(8,128)(2,1)} %own_ref.3, bf16[4,256,1024]{2,1,0:T(8,128)(2,1)} %get-tuple-element.12.sib_ref, f32[8,2,512]{2,1,0:T(2,128)} %reshape.63.mask_ref, ...), custom_call_target="tpu_custom_call" | custom-call | tf_op jit(solution)/shard_map/pallas_call | solution.py:291
  148.8 77.6 %shard_map.72 = f32[2,32,256]{2,1,0:T(8,128)} custom-call(bf16[8,8,4,32,256]{4,3,2,1,0:T(8,128)(2,1)} %bitcast.15, bf16[8,8,4,32,256]{4,3,2,1,0:T(8,128)(2,1)} %bitcast.16), custom_call_target="tpu_custom_call" | custom-call | tf_op jit(solution)/shard_map/pallas_call | solution.py:535
  226.5 0.8 convert_bitcast_fusion
  227.3 0.6 copy.31
  (5 shorter events, 0.1 us)

commit v2 on v0

v2 whole, which is shorter than its diff:
```python
import functools
import heapq
import itertools
import math

import jax
import jax.numpy as jnp
from jax import lax
from jax.experimental import pallas as pl
from jax.experimental.pallas import tpu as pltpu
from jax.sharding import PartitionSpec as P

BLK = 128
CORES = 2
X_CHIPS = 4
VMEM_LIMIT = 60 * 1024 * 1024
NEG_FILL = -1e30
MESH = pl.DeviceIdType.MESH
LINK_RATE = 51e3
LINK_DELAY = 1.5
ISSUE = 0.1
LOGITS_COST = 1.5
GRADS_COST = 1.2


class Place:
    def __init__(self, y_count, z_count, x_count):
        dp, lab = lax.axis_index("dp"), lax.axis_index("label")
        self.dp, self.lab = dp, lab
        self.y, self.core = dp // CORES, dp % CORES
        self.z, self.x = lab // x_count, lab % x_count
        self.count = {"y": y_count, "z": z_count, "x": x_count}
        self.pos = {"y": self.y, "z": self.z, "x": self.x}

    def at(self, axis, offset):
        n = self.count[axis]
        return lax.rem(self.pos[axis] + (offset % n), n)

    def device(self, axis, offset):
        if axis == "core":
            return (self.y * CORES + (1 - self.core), self.lab)
        p = self.at(axis, offset)
        if axis == "y":
            return (p * CORES + self.core, self.lab)
        if axis == "z":
            return (self.dp, p * self.count["x"] + self.x)
        return (self.dp, self.z * self.count["x"] + p)


def greet(devices):
    barrier = pltpu.get_barrier_semaphore()
    for device in devices:
        pl.semaphore_signal(barrier, inc=1, device_id=device, device_id_type=MESH)
    pl.semaphore_wait(barrier, len(devices))


class Engine:
    def __init__(self, place, send_sem, recv_sem):
        self.place, self.send_sem, self.recv_sem = place, send_sem, recv_sem
        self.ids, self.order = itertools.count(), itertools.count()
        self.sent, self.heap, self.ready = [], [], []
        self.free, self.now = {}, 0.0

    def send(self, axis, offset, src, dst, arrived):
        i = next(self.ids)
        copy = pltpu.make_async_remote_copy(
            src_ref=src,
            dst_ref=dst,
            send_sem=self.send_sem.at[i],
            recv_sem=self.recv_sem.at[i],
            device_id=self.place.device(axis, offset),
            device_id_type=MESH,
        )
        copy.start()
        self.sent.append(copy)
        hops, sign, rate = 1, 1, 6 * LINK_RATE
        if axis != "core":
            n = self.place.count[axis]
            offset = offset % n
            sign = 1 if offset <= n // 2 else -1
            hops, rate = min(offset, n - offset), LINK_RATE
        size = math.prod(src.shape) * jnp.dtype(src.dtype).itemsize
        start = max(self.now, self.free.get((axis, sign), 0.0))
        self.free[axis, sign] = start + hops * size / rate
        heapq.heappush(
            self.heap, (self.free[axis, sign] + LINK_DELAY, next(self.order), copy, arrived)
        )
        self.now += ISSUE

    def work(self, cost, run):
        self.ready.append((cost, run))

    def run(self):
        while self.heap or self.ready:
            if self.ready and (not self.heap or self.heap[0][0] > self.now):
                cost, run = self.ready.pop(0)
                run()
                self.now += cost
                continue
            when, _, copy, arrived = heapq.heappop(self.heap)
            self.now = max(self.now, when) + ISSUE
            copy.wait_recv()
            arrived()
        for copy in self.sent:
            copy.wait_send()


def countdown(count, run):
    left = [count]

    def one():
        left[0] -= 1
        if left[0] == 0:
            run()

    return one


def reach(n, sign, half):
    return n // 2 if (sign > 0) == (half == 0) else n // 2 - 1


def spread(engine, axis, half, source, target, arrived):
    place = engine.place
    n = place.count[axis]

    def step(sign, k):
        origin = place.at(axis, -sign * (k - 1))
        src = source() if k == 1 else target(origin)
        engine.send(axis, sign, src, target(origin), lambda: landed(sign, k))

    def landed(sign, k):
        if k + 1 <= reach(n, sign, half):
            step(sign, k + 1)
        arrived(-sign * k % n)

    for sign in (1, -1):
        if reach(n, sign, half) >= 1:
            step(sign, 1)


def add_into(total, term):
    def one(i, carry):
        value = total[i].astype(jnp.float32) + term[i].astype(jnp.float32)
        total[i] = value.astype(total.dtype)
        return carry

    lax.fori_loop(0, total.shape[0], one, 0)


def ring_sum(engine, axis, half, own, slots, total, done):
    place = engine.place
    n = place.count[axis]
    chains = [(sign, reach(n, sign, half)) for sign in (1, -1) if reach(n, sign, half) > 0]

    def finish():
        parts = [slots[sign, half].at[length - 1] for sign, length in chains]
        first = own(place.at(axis, 0))

        def one(i, carry):
            value = first[i].astype(jnp.float32)
            for part in parts:
                value = value + part[i].astype(jnp.float32)
            total[i] = value
            return carry

        lax.fori_loop(0, total.shape[0], one, 0)
        done()

    landed = countdown(len(chains), lambda: engine.work(0.3, finish))

    def step(sign, length, k):
        if k == length:
            landed()
            return
        ref = own(place.at(axis, sign * (length - k)))
        if k > 0:
            add_into(slots[sign, half].at[k - 1], ref)
            engine.now += 0.3
            ref = slots[sign, half].at[k - 1]
        engine.send(axis, sign, ref, slots[sign, half].at[k], lambda: step(sign, length, k + 1))

    for sign, length in chains:
        step(sign, length, 0)


def direct_sum(engine, axis, total, slots, out):
    place = engine.place
    n = place.count[axis]

    def finish():
        value = total[place.at(axis, 0)]
        for o in range(1, n):
            value = value + slots[o - 1]
        out[...] = value

    landed = countdown(n - 1, lambda: engine.work(0.2, finish))
    for o in range(1, n):
        engine.send(axis, o, total.at[place.at(axis, o)], slots.at[o - 1], landed)


def merge(parts):
    high = parts[0][0:1]
    for part in parts[1:]:
        high = jnp.maximum(high, part[0:1])
    total = sum(part[1:2] * jnp.exp(part[0:1] - high) for part in parts)
    hits = sum(part[2:3] for part in parts)
    return high, total, hits


def write(ref, values):
    for row, value in enumerate(values):
        ref[row : row + 1, :] = value


UNIT = 16
SHARES = {"x": 3, "z": 3, "y": 2}


def plan(sizes, inst, width, size, stored, pos_count):
    n = dict(zip("yzx", sizes))
    y, z, x = sizes
    bf, f4 = jnp.bfloat16, jnp.float32
    tile = (8, inst)
    rows = {c: SHARES[c] * UNIT for c in SHARES}
    buffers = {
        "f_all": ((y, inst, width), bf),
        "p_all": ((y, pos_count, inst), jnp.int32),
        "rows_all": ((CORES * stored, size, width), bf),
        "turned": ((CORES * stored, width, size), bf),
        "kept": ((y, CORES, size, inst), f4),
        "hits": ((y, CORES, size, inst), bf),
        "peaks": ((y, CORES) + tile, f4),
        "stats": ((y,) + tile, f4),
        "lse_all": ((y,) + tile, f4),
        "held": ((3,) + tile, f4),
        "stat_y": ((y - 1,) + tile, f4),
        "stat_x": ((x - 1,) + tile, f4),
        "stat_z": ((z - 1,) + tile, f4),
        "g_x": ((y, z, x, rows["x"], BLK), bf),
        "g_z": ((y, z, x, rows["z"], BLK), bf),
        "g_y": ((y, z, x, rows["y"], BLK), bf),
        "x_sum": ((y, z, rows["x"], BLK), f4),
        "xy_sum": ((z, rows["x"], BLK), f4),
        "z_sum": ((y, x, rows["z"], BLK), f4),
        "zx_sum": ((y, rows["z"], BLK), f4),
        "y_sum": ((z, x, rows["y"], BLK), f4),
        "yx_sum": ((z, rows["y"], BLK), f4),
        "last_x": ((z - 1, rows["x"], BLK), f4),
        "last_z": ((y - 1, rows["z"], BLK), f4),
        "last_y": ((z - 1, rows["y"], BLK), f4),
    }
    rings = {
        "x1": ("x", (y // 2, z, rows["x"], BLK), bf),
        "z1": ("z", (y // 2, x, rows["z"], BLK), bf),
        "y1": ("y", (z // 2, x, rows["y"], BLK), bf),
        "x2": ("y", (z // 2, rows["x"], BLK), f4),
        "z2": ("x", (y // 2, rows["z"], BLK), f4),
        "y2": ("x", (z // 2, rows["y"], BLK), f4),
    }
    copies = 1 + 2 * (z - 1) + (y - 1)
    for name, (axis, shape, dtype) in rings.items():
        for sign in (1, -1):
            for half in (0, 1):
                steps = reach(n[axis], sign, half)
                copies += steps
                buffers[name, sign, half] = ((max(steps, 1),) + shape, dtype)
    copies += (y - 1) * (5 + (x - 1) + (z - 1)) + 2 * (y - 1) + (x - 1) + (z - 1)
    return buffers, copies


def step_kernel(sizes, names, pick, cluster, feats, pos, rows, mask, loss, out_x, out_z, out_y, *scratch):
    y_count, z_count, x_count = sizes
    place = Place(*sizes)
    b = dict(zip(names, scratch))
    local_sem, send_sem, recv_sem = scratch[len(names) :]
    inst, width = feats.shape
    stored, size, _ = rows.shape
    pos_count = pos.shape[0]
    y_half, z_half = y_count // 2, z_count // 2
    f_all, p_all, rows_all, turned = b["f_all"], b["p_all"], b["rows_all"], b["turned"]
    kept, hits, peaks, stats, lse_all, held = (
        b[k] for k in ("kept", "hits", "peaks", "stats", "lse_all", "held")
    )
    locals_ = [
        pltpu.make_async_copy(rows, rows_all.at[pl.ds(0, stored)], local_sem.at[0]),
        pltpu.make_async_copy(feats, f_all.at[place.y], local_sem.at[1]),
        pltpu.make_async_copy(pos, p_all.at[place.y], local_sem.at[2]),
    ]
    for copy in locals_:
        copy.start()
    greet(
        [
            place.device(axis, offset)
            for axis, n in (("y", y_count), ("x", x_count), ("z", z_count))
            for offset in range(1, n)
        ]
        + [place.device("core", 1)]
    )
    engine = Engine(place, send_sem, recv_sem)

    def logits_of(offset):
        def run():
            d = place.at("y", offset)

            def one(s, carry):
                logits = lax.dot_general(
                    rows_all[s * stored + pick[d, s]],
                    f_all[d],
                    (((1,), (1,)), ((), ())),
                    preferred_element_type=jnp.float32,
                )
                label = cluster[d, s] * size + lax.broadcasted_iota(jnp.int32, logits.shape, 0)
                hit = p_all[d, 0:1, :] == label
                for p in range(1, pos_count):
                    hit = hit | (p_all[d, p : p + 1, :] == label)
                hits[d, s] = jnp.where(hit, 1.0 / pos_count, 0.0).astype(jnp.bfloat16)
                valid = jnp.where(mask[d, pl.ds(s, 1), :] > 0, logits, NEG_FILL)
                high = jnp.max(valid, axis=0, keepdims=True)
                power = jnp.exp(valid - high)
                kept[d, s] = power
                peak = peaks.at[d, s]
                peak[0:1, :] = high
                peak[1:2, :] = jnp.sum(power, axis=0, keepdims=True)
                peak[2:3, :] = jnp.sum(jnp.where(hit, logits, 0.0), axis=0, keepdims=True)
                return carry

            lax.fori_loop(0, CORES, one, 0)
            stats[d] = jnp.zeros_like(stats[d])
            write(stats.at[d], merge([peaks[d, s] for s in range(CORES)]))
            if offset % y_count:
                engine.send("y", offset, stats.at[d], b["stat_y"].at[offset - 1], stat_landed)
            else:
                stat_landed()

        return run

    def over_y():
        write(
            held.at[0],
            merge([stats[place.y]] + [b["stat_y"][o] for o in range(y_count - 1)]),
        )
        landed = countdown(x_count - 1, lambda: engine.work(0.2, over_x))
        for o in range(1, x_count):
            engine.send("x", o, held.at[0], b["stat_x"].at[o - 1], landed)

    def over_x():
        write(held.at[1], merge([held[0]] + [b["stat_x"][o] for o in range(x_count - 1)]))
        landed = countdown(z_count - 1, lambda: engine.work(0.2, over_z))
        for o in range(1, z_count):
            engine.send("z", o, held.at[1], b["stat_z"].at[o - 1], landed)

    def over_z():
        high, total, found = merge([held[1]] + [b["stat_z"][o] for o in range(z_count - 1)])
        lse = high + jnp.log(total)
        held[2] = jnp.broadcast_to(lse, held.shape[1:])
        landed = countdown(y_count - 1, queue_grads)
        for o in range(1, y_count):
            engine.send("y", o, held.at[2], lse_all.at[place.y], landed)
        loss[...] = jnp.broadcast_to(lse - found / pos_count, loss.shape)
        lse_all[place.y] = held[2]

    stat_landed = countdown(y_count, lambda: engine.work(0.2, over_y))

    def grads_of(half):
        def run():
            def one(i, carry):
                d = half * y_half + i
                shares = None
                lse = lse_all[d, 0:1, :]
                for s in range(CORES):
                    scale = jnp.exp(peaks[d, s, 0:1, :] - lse)
                    dlogit = kept[d, s] * scale - hits[d, s].astype(jnp.float32)
                    term = jnp.dot(
                        turned[s * stored + pick[d, s]],
                        dlogit.astype(jnp.bfloat16),
                        preferred_element_type=jnp.float32,
                    )
                    shares = term if shares is None else shares + term
                shares = shares.astype(jnp.bfloat16).reshape(z_count, x_count, 2 * UNIT, inst)
                b["g_x"][d, :, :, : 2 * UNIT] = shares[..., :BLK]
                b["g_x"][d, :, :, 2 * UNIT :] = shares[:, :, :UNIT, BLK : 2 * BLK]
                b["g_z"][d, :, :, :UNIT] = shares[:, :, UNIT:, BLK : 2 * BLK]
                b["g_z"][d, :, :, UNIT:] = shares[..., 2 * BLK : 3 * BLK]
                b["g_y"][d] = shares[..., 3 * BLK :]
                return carry

            lax.fori_loop(0, y_half, one, 0)
            start_sums(half)

        return run

    def queue_grads():
        for half in (0, 1):
            engine.work(y_half * GRADS_COST, grads_of(half))

    def slots(name):
        return {(sign, half): b[name, sign, half] for sign in (1, -1) for half in (0, 1)}

    def part(half, count):
        return pl.ds(half * count, count)

    def second_x():
        for half in (0, 1):
            ring_sum(
                engine,
                "y",
                half,
                lambda dest, half=half: b["x_sum"].at[dest, part(half, z_half)],
                slots("x2"),
                b["xy_sum"].at[part(half, z_half)],
                last_x,
            )

    last_x = countdown(2, lambda: direct_sum(engine, "z", b["xy_sum"], b["last_x"], out_x))
    last_z = countdown(2, lambda: direct_sum(engine, "y", b["zx_sum"], b["last_z"], out_z))
    last_y = countdown(2, lambda: direct_sum(engine, "z", b["yx_sum"], b["last_y"], out_y))
    first_x = countdown(2, second_x)

    def start_sums(half):
        ring_sum(
            engine,
            "z",
            half,
            lambda dest: b["g_z"].at[part(half, y_half), dest],
            slots("z1"),
            b["z_sum"].at[part(half, y_half)],
            lambda: ring_sum(
                engine,
                "x",
                half,
                lambda dest: b["z_sum"].at[part(half, y_half), dest],
                slots("z2"),
                b["zx_sum"].at[part(half, y_half)],
                last_z,
            ),
        )
        ring_sum(
            engine,
            "x",
            half,
            lambda dest: b["g_x"].at[part(half, y_half), :, dest],
            slots("x1"),
            b["x_sum"].at[part(half, y_half)],
            first_x,
        )
        if half == 0:
            return
        for zh in (0, 1):
            ring_sum(
                engine,
                "y",
                zh,
                lambda dest, zh=zh: b["g_y"].at[dest, part(zh, z_half)],
                slots("y1"),
                b["y_sum"].at[part(zh, z_half)],
                lambda zh=zh: ring_sum(
                    engine,
                    "x",
                    zh,
                    lambda dest: b["y_sum"].at[part(zh, z_half), dest],
                    slots("y2"),
                    b["yx_sum"].at[part(zh, z_half)],
                    last_y,
                ),
            )

    a_part, b_part = inst // 2 // x_count, inst // 4 // z_count
    a_from, b_from = inst // 4, 3 * inst // 4
    c_part = inst // 8
    turn = itertools.count()
    complete = {
        o: countdown(x_count + z_count + 3, lambda o=o: engine.work(LOGITS_COST, logits_of(o)))
        for o in range(1, y_count)
    }

    def cut(origin, start, count):
        return f_all.at[origin, pl.ds(pl.multiple_of(start, 16), count)]

    def a_landed(o):
        origin = place.at("y", o)
        complete[o]()
        spread(
            engine,
            "x",
            next(turn) % 2,
            lambda: cut(origin, a_from + place.x * a_part, a_part),
            lambda p: cut(origin, a_from + p * a_part, a_part),
            lambda _: complete[o](),
        )

    def b_landed(o):
        origin = place.at("y", o)
        complete[o]()
        spread(
            engine,
            "z",
            next(turn) % 2,
            lambda: cut(origin, b_from + place.z * b_part, b_part),
            lambda p: cut(origin, b_from + p * b_part, b_part),
            lambda _: complete[o](),
        )

    def from_feats(start, count):
        return lambda: feats.at[pl.ds(pl.multiple_of(start, 16), count)]

    def turn_rows(base):
        def run():
            def one(i, carry):
                turned[base + i] = rows_all[base + i].T
                return carry

            lax.fori_loop(0, stored, one, 0)

        return run

    def swapped():
        engine.work(LOGITS_COST, logits_of(0))
        engine.work(3.0, turn_rows(stored))

    start = a_from + place.x * a_part
    spread(
        engine, "y", 0, from_feats(start, a_part),
        lambda p, start=start: cut(p, start, a_part), a_landed,
    )
    start = b_from + place.z * b_part
    spread(
        engine, "y", 1, from_feats(start, b_part),
        lambda p, start=start: cut(p, start, b_part), b_landed,
    )
    engine.send("core", 1, rows, rows_all.at[pl.ds(stored, stored)], swapped)
    for o in range(1, y_count):
        engine.send("y", o, pos, p_all.at[place.y], complete[-o % y_count])
    for half in (0, 1):
        spread(
            engine, "y", half, from_feats(half * c_part, c_part),
            lambda p, half=half: cut(p, half * c_part, c_part), lambda o: complete[o](),
        )
    for copy in locals_:
        copy.wait()
    engine.work(3.0, turn_rows(0))
    engine.run()


def step(sizes, pick, cluster, feats, pos, rows, mask):
    inst, width = feats.shape
    stored, size, _ = rows.shape
    buffers, copies = plan(sizes, inst, width, size, stored, pos.shape[0])
    scratch = [pltpu.VMEM(*spec) for spec in buffers.values()]
    scratch += [pltpu.SemaphoreType.DMA((n,)) for n in (3, copies, copies)]
    return pl.pallas_call(
        functools.partial(step_kernel, sizes, list(buffers)),
        out_shape=[jax.ShapeDtypeStruct((8, inst), jnp.float32)]
        + [jax.ShapeDtypeStruct((SHARES[c] * UNIT, BLK), jnp.float32) for c in "xzy"],
        in_specs=[pl.BlockSpec(memory_space=pltpu.SMEM)] * 2
        + [pl.BlockSpec(memory_space=pl.ANY)] * 3
        + [pl.BlockSpec(memory_space=pltpu.VMEM)],
        out_specs=[pl.BlockSpec(memory_space=pltpu.VMEM)] * 4,
        scratch_shapes=scratch,
        compiler_params=pltpu.CompilerParams(
            collective_id=0, has_side_effects=True, vmem_limit_bytes=VMEM_LIMIT
        ),
    )(pick, cluster, feats, pos, rows, mask)


def shards(x_count, feats, weights, shortlist, slot_of, positives):
    y_count = lax.axis_size("dp") // CORES
    lab_count = lax.axis_size("label")
    sizes = (y_count, lab_count // x_count, x_count)
    dp_index, lab_index = lax.axis_index("dp"), lax.axis_index("label")
    core = dp_index % CORES
    stored, size, width = weights.shape
    inst, pos_count = positives.shape
    block_count = inst // BLK
    half_blocks = block_count // 2
    pair = jnp.stack([dp_index, dp_index + 1 - 2 * core]) * lab_count + lab_index
    slots = (pair[:, None] * stored + jnp.arange(stored, dtype=jnp.int32)).reshape(-1)
    ids = jnp.arange(slot_of.shape[0], dtype=jnp.int32)
    clusters = jnp.sum(jnp.where(slots[:, None] == slot_of[None, :], ids[None, :], 0), axis=1)
    lists = shortlist.reshape(y_count, CORES, block_count, -1)
    lists = lax.dynamic_index_in_dim(lists, core, 1, keepdims=False)
    member = jnp.any(lists[:, :, None, :] == clusters[None, None, :, None], axis=3)
    member = member.reshape(y_count, block_count, CORES, stored).astype(jnp.int32)
    chosen = jnp.sum(member[:, :half_blocks], axis=1)
    pick = jnp.sum(chosen * jnp.arange(stored, dtype=jnp.int32), axis=2)
    cluster = jnp.sum(chosen * clusters.reshape(1, CORES, stored), axis=2)
    mask = jnp.sum(member, axis=3).astype(jnp.float32).transpose(0, 2, 1)
    mask = jnp.broadcast_to(mask[..., None], mask.shape + (BLK,)).reshape(y_count, CORES, inst)

    loss, share_x, share_z, share_y = step(sizes, pick, cluster, feats, positives.T, weights, mask)
    lanes = [
        share_x[: 2 * UNIT],
        jnp.concatenate([share_x[2 * UNIT :], share_z[:UNIT]]),
        share_z[UNIT:],
        share_y,
    ]
    grads = jnp.concatenate(lanes, axis=1).T
    return loss[0], grads.astype(jnp.bfloat16)


def solution(mesh, x_count=X_CHIPS):
    in_specs = (P("dp", None), P(("dp", "label"), None, None), P(), P(), P("dp", None))
    out_specs = (P("dp"), P("dp", "label"))
    return jax.shard_map(
        functools.partial(shards, x_count),
        mesh=mesh,
        in_specs=in_specs,
        out_specs=out_specs,
        check_vma=False,
    )
```

time: 980 us -> 160 us (0.16)
  waiting for transfers between devices: 401 us -> 0 us
  other arithmetic: 186 us -> 4.7 us
  local copies, waits for them, and re-layouts: 162 us -> 4.59 us
  Pallas kernels: 0 us -> 150 us
  blocking collectives: 147 us -> 0 us
  matrix products: 55.2 us -> 0 us
  between operations: 14.3 us -> 0.69 us
    reduce_scatter x1 -> x0, waiting for transfers between devices: 218 us -> none  [shards(): lax.psum_scatter(partial_grad, 'label', scatter_dimension=1, tiled=True)]
    all_to_all x1 -> x0, waiting for transfers between devices: 183 us -> none  [shards(): lax.all_to_all(outgoing, 'dp', split_axis=0, concat_axis=0, tiled=True)]
    pallas_call x0 -> x1, Pallas kernels: none -> 150 us  [step(): pl.pallas_call(functools.partial(step_kernel, sizes, list(buffers)), out_...]
    gather x68 -> x0, local copies, waits for them, and re-layouts: 106 us -> none  [the longest x3 45.6 us: shards(): first_slots = jnp.take(slot_of, first_half)]
    reduce_sum x52 -> x4, other arithmetic: 94.9 us -> 1.02 us  [the longest x1 0.89 us: shards(): jnp.sum(jnp.where(slots[:, None] == slot_of[None, :], ids[None, :], 0), a...]
    psum x1 -> x0, blocking collectives: 74.3 us -> none  [shards(): totals, pos_total = lax.psum((exp_local, pos_local), 'label')]
    pmax x1 -> x0, blocking collectives: 72.8 us -> none  [shards(): highest = lax.pmax(local_max.reshape(-1), 'label')]
    dot_general x32 -> x0, matrix products: 55.2 us -> none  [the longest x16 33.6 us: slot_logits(): jnp.einsum('id,od->io', pair_rows, rows_in, preferred_element_type=jnp.fl...]
  transfers between devices with their start and end apart: 2 -> 0, of which waited for: 2 -> 0; matrix products, arithmetic and copies ran while one was open for 0% -> 0% of each run, Pallas kernels for 0% -> 0%
where the time goes in v2:
time: 160 us
  Pallas kernels  150 us (94%)
  other arithmetic  4.7 us (3%)
  local copies, waits for them, and re-layouts  4.59 us (3%)
    pallas_call x1, Pallas kernels, step(): pl.pallas_call(functools.partial(step_kernel, sizes, list(buffers)), out_...  150 us

profile of v2, /device:TPU:6, one launch (start us, length us, event | category | flops | bytes accessed | tf_op | source)
XLA Modules:
  0.0 159.9 jit_solution(5676308035097591211)
XLA Ops:
  0.6 0.1 fusion.1
  0.7 0.1 iota_add_fusion
  0.8 0.1 add.49
  0.9 0.9 select_reduce_fusion
  1.8 0.1 mul.41
  1.9 0.9 reshape.54
  2.7 0.7 compare_reduce_fusion
  3.5 0.1 copy.16
  3.6 0.1 multiply_reduce_fusion
  3.7 0.7 copy.19.cluster
  4.3 0.1 copy.17
  4.4 0.7 copy.18.pick
  5.1 0.1 broadcast_in_dim.16
  5.2 0.7 reshape.55.mask
  5.8 149.9 %shard_map.68 = (f32[8,512]{1,0:T(8,128)}, f32[48,128]{1,0:T(8,128)}, f32[48,128]{1,0:T(8,128)}, f32[32,128]{1,0:T(8,128)}) custom-call(s32[8,2]{1,0:T(8,128)} %copy.18.pick, s32[8,2]{1,0:T(8,128)} %copy.19.cluster, bf16[512,1024]{1,0:T(8,128)(2,1)} %feats.1, s32[8,512]{1,0:T(8,128)} %bitcast.13, bf16[4,256,1024]{2,1,0:T(8,128)(2,1)} %rows.1, ...), custom_call_target="tpu_custom_call" | custom-call | tf_op jit(solution)/shard_map/pallas_call | solution.py:551
  155.7 1.3 slice.23
  157.0 0.7 convert.19
  157.7 0.7 convert.17
  158.5 0.7 convert.18
  159.2 0.6 maximum_bitcast_fusion
  (9 shorter events, 0.1 us)

commit v3 on v2

--- a/solution.py
+++ b/solution.py
@@ -16,8 +16,10 @@
 VMEM_LIMIT = 60 * 1024 * 1024
 NEG_FILL = -1e30
 MESH = pl.DeviceIdType.MESH
+A_PARTS, B_PARTS, C_PARTS = 16, 16, 0
+FAR = {"y": 1, "z": 1, "x": 1}
 LINK_RATE = 51e3
-LINK_DELAY = 1.5
+LINK_DELAY = 2.5
 ISSUE = 0.1
 LOGITS_COST = 1.5
 GRADS_COST = 1.2
@@ -94,8 +96,8 @@
         while self.heap or self.ready:
             if self.ready and (not self.heap or self.heap[0][0] > self.now):
                 cost, run = self.ready.pop(0)
+                self.now += cost
                 run()
-                self.now += cost
                 continue
             when, _, copy, arrived = heapq.heappop(self.heap)
             self.now = max(self.now, when) + ISSUE
@@ -124,19 +126,23 @@
     place = engine.place
     n = place.count[axis]
 
-    def step(sign, k):
-        origin = place.at(axis, -sign * (k - 1))
-        src = source() if k == 1 else target(origin)
-        engine.send(axis, sign, src, target(origin), lambda: landed(sign, k))
+    far = FAR[axis]
+
+    def pass_on(sign, k):
+        origin = place.at(axis, -sign * k)
+        src = target(origin) if k else source()
+        for hops in range(1, min(far, reach(n, sign, half) - k) + 1):
+            engine.send(
+                axis, sign * hops, src, target(origin), lambda hops=hops: landed(sign, k + hops)
+            )
 
     def landed(sign, k):
-        if k + 1 <= reach(n, sign, half):
-            step(sign, k + 1)
+        if k % far == 0:
+            pass_on(sign, k)
         arrived(-sign * k % n)
 
     for sign in (1, -1):
-        if reach(n, sign, half) >= 1:
-            step(sign, 1)
+        pass_on(sign, 0)
 
 
 def add_into(total, term):
@@ -184,7 +190,7 @@
         step(sign, length, 0)
 
 
-def direct_sum(engine, axis, total, slots, out):
+def direct_sum(engine, axis, first, total, slots, out):
     place = engine.place
     n = place.count[axis]
 
@@ -192,36 +198,60 @@
         value = total[place.at(axis, 0)]
         for o in range(1, n):
             value = value + slots[o - 1]
-        out[...] = value
+        for place_in, rows_in, lanes_in in spots(first):
+            out[rows_in, lanes_in] = value[place_in].astype(out.dtype)
 
     landed = countdown(n - 1, lambda: engine.work(0.2, finish))
     for o in range(1, n):
         engine.send(axis, o, total.at[place.at(axis, o)], slots.at[o - 1], landed)
 
 
-def merge(parts):
-    high = parts[0][0:1]
+def merge(parts, n):
+    high = parts[0][0:n]
     for part in parts[1:]:
-        high = jnp.maximum(high, part[0:1])
-    total = sum(part[1:2] * jnp.exp(part[0:1] - high) for part in parts)
-    hits = sum(part[2:3] for part in parts)
+        high = jnp.maximum(high, part[0:n])
+    total = sum(part[n : 2 * n] * jnp.exp(part[0:n] - high) for part in parts)
+    hits = sum(part[2 * n : 3 * n] for part in parts)
     return high, total, hits
 
 
 def write(ref, values):
-    for row, value in enumerate(values):
-        ref[row : row + 1, :] = value
+    row = 0
+    for value in values:
+        ref[row : row + value.shape[0], :] = value
+        row += value.shape[0]
+
+
+def folded(row):
+    return [row[:, i : i + BLK] for i in range(0, row.shape[1], BLK)]
+
+
+def unfolded(rows):
+    return jnp.concatenate([rows[i : i + 1] for i in range(rows.shape[0])], axis=1)
 
 
 UNIT = 16
+UNITS = [(lane, rows) for lane in range(4) for rows in range(2)]
 SHARES = {"x": 3, "z": 3, "y": 2}
+
+
+def units(axis):
+    first = {"x": 0, "z": SHARES["x"], "y": SHARES["x"] + SHARES["z"]}[axis]
+    return UNITS[first : first + SHARES[axis]]
+
+
+def spots(axis):
+    for i, (lane, rows) in enumerate(units(axis)):
+        yield slice(i * UNIT, i * UNIT + UNIT), slice(rows * UNIT, rows * UNIT + UNIT), slice(
+            lane * BLK, lane * BLK + BLK
+        )
 
 
 def plan(sizes, inst, width, size, stored, pos_count):
     n = dict(zip("yzx", sizes))
     y, z, x = sizes
     bf, f4 = jnp.bfloat16, jnp.float32
-    tile = (8, inst)
+    tile, lse_tile = (4 * inst // BLK, BLK), (8, BLK)
     rows = {c: SHARES[c] * UNIT for c in SHARES}
     buffers = {
         "f_all": ((y, inst, width), bf),
@@ -232,8 +262,9 @@
         "hits": ((y, CORES, size, inst), bf),
         "peaks": ((y, CORES) + tile, f4),
         "stats": ((y,) + tile, f4),
-        "lse_all": ((y,) + tile, f4),
-        "held": ((3,) + tile, f4),
+        "lse_all": ((y,) + lse_tile, f4),
+        "lse_mine": (lse_tile, f4),
+        "held": ((2,) + tile, f4),
         "stat_y": ((y - 1,) + tile, f4),
         "stat_x": ((x - 1,) + tile, f4),
         "stat_z": ((z - 1,) + tile, f4),
@@ -269,7 +300,7 @@
     return buffers, copies
 
 
-def step_kernel(sizes, names, pick, cluster, feats, pos, rows, mask, loss, out_x, out_z, out_y, *scratch):
+def step_kernel(sizes, names, pick, cluster, feats, pos, rows, mask, loss, out, *scratch):
     y_count, z_count, x_count = sizes
     place = Place(*sizes)
     b = dict(zip(names, scratch))
@@ -279,9 +310,10 @@
     pos_count = pos.shape[0]
     y_half, z_half = y_count // 2, z_count // 2
     f_all, p_all, rows_all, turned = b["f_all"], b["p_all"], b["rows_all"], b["turned"]
-    kept, hits, peaks, stats, lse_all, held = (
-        b[k] for k in ("kept", "hits", "peaks", "stats", "lse_all", "held")
+    kept, hits, peaks, stats, lse_all, lse_mine, held = (
+        b[k] for k in ("kept", "hits", "peaks", "stats", "lse_all", "lse_mine", "held")
     )
+    blocks = inst // BLK
     locals_ = [
         pltpu.make_async_copy(rows, rows_all.at[pl.ds(0, stored)], local_sem.at[0]),
         pltpu.make_async_copy(feats, f_all.at[place.y], local_sem.at[1]),
@@ -319,15 +351,14 @@
                 high = jnp.max(valid, axis=0, keepdims=True)
                 power = jnp.exp(valid - high)
                 kept[d, s] = power
-                peak = peaks.at[d, s]
-                peak[0:1, :] = high
-                peak[1:2, :] = jnp.sum(power, axis=0, keepdims=True)
-                peak[2:3, :] = jnp.sum(jnp.where(hit, logits, 0.0), axis=0, keepdims=True)
+                total = jnp.sum(power, axis=0, keepdims=True)
+                found = jnp.sum(jnp.where(hit, logits, 0.0), axis=0, keepdims=True)
+                write(peaks.at[d, s], folded(high) + folded(total) + folded(found))
                 return carry
 
             lax.fori_loop(0, CORES, one, 0)
             stats[d] = jnp.zeros_like(stats[d])
-            write(stats.at[d], merge([peaks[d, s] for s in range(CORES)]))
+            write(stats.at[d], merge([peaks[d, s] for s in range(CORES)], blocks))
             if offset % y_count:
                 engine.send("y", offset, stats.at[d], b["stat_y"].at[offset - 1], stat_landed)
             else:
@@ -336,29 +367,32 @@
         return run
 
     def over_y():
+        held[0] = jnp.zeros_like(held[0])
         write(
             held.at[0],
-            merge([stats[place.y]] + [b["stat_y"][o] for o in range(y_count - 1)]),
+            merge([stats[place.y]] + [b["stat_y"][o] for o in range(y_count - 1)], blocks),
         )
         landed = countdown(x_count - 1, lambda: engine.work(0.2, over_x))
         for o in range(1, x_count):
             engine.send("x", o, held.at[0], b["stat_x"].at[o - 1], landed)
 
     def over_x():
-        write(held.at[1], merge([held[0]] + [b["stat_x"][o] for o in range(x_count - 1)]))
+        held[1] = jnp.zeros_like(held[1])
+        write(held.at[1], merge([held[0]] + [b["stat_x"][o] for o in range(x_count - 1)], blocks))
         landed = countdown(z_count - 1, lambda: engine.work(0.2, over_z))
         for o in range(1, z_count):
             engine.send("z", o, held.at[1], b["stat_z"].at[o - 1], landed)
 
     def over_z():
-        high, total, found = merge([held[1]] + [b["stat_z"][o] for o in range(z_count - 1)])
+        high, total, found = merge([held[1]] + [b["stat_z"][o] for o in range(z_count - 1)], blocks)
         lse = high + jnp.log(total)
-        held[2] = jnp.broadcast_to(lse, held.shape[1:])
+        lse_mine[...] = jnp.zeros_like(lse_mine)
+        write(lse_mine, [lse])
         landed = countdown(y_count - 1, queue_grads)
         for o in range(1, y_count):
-            engine.send("y", o, held.at[2], lse_all.at[place.y], landed)
-        loss[...] = jnp.broadcast_to(lse - found / pos_count, loss.shape)
-        lse_all[place.y] = held[2]
+            engine.send("y", o, lse_mine, lse_all.at[place.y], landed)
+        loss[...] = lse - found / pos_count
+        lse_all[place.y] = lse_mine[...]
 
     stat_landed = countdown(y_count, lambda: engine.work(0.2, over_y))
 
@@ -367,9 +401,9 @@
             def one(i, carry):
                 d = half * y_half + i
                 shares = None
-                lse = lse_all[d, 0:1, :]
+                lse = lse_all[d][:blocks]
                 for s in range(CORES):
-                    scale = jnp.exp(peaks[d, s, 0:1, :] - lse)
+                    scale = unfolded(jnp.exp(peaks[d, s][:blocks] - lse))
                     dlogit = kept[d, s] * scale - hits[d, s].astype(jnp.float32)
                     term = jnp.dot(
                         turned[s * stored + pick[d, s]],
@@ -378,11 +412,9 @@
                     )
                     shares = term if shares is None else shares + term
                 shares = shares.astype(jnp.bfloat16).reshape(z_count, x_count, 2 * UNIT, inst)
-                b["g_x"][d, :, :, : 2 * UNIT] = shares[..., :BLK]
-                b["g_x"][d, :, :, 2 * UNIT :] = shares[:, :, :UNIT, BLK : 2 * BLK]
-                b["g_z"][d, :, :, :UNIT] = shares[:, :, UNIT:, BLK : 2 * BLK]
-                b["g_z"][d, :, :, UNIT:] = shares[..., 2 * BLK : 3 * BLK]
-                b["g_y"][d] = shares[..., 3 * BLK :]
+                for axis, share in (("x", b["g_x"]), ("z", b["g_z"]), ("y", b["g_y"])):
+                    for place_in, rows_in, lanes_in in spots(axis):
+                        share[d, :, :, place_in] = shares[:, :, rows_in, lanes_in]
                 return carry
 
             lax.fori_loop(0, y_half, one, 0)
@@ -412,9 +444,9 @@
                 last_x,
             )
 
-    last_x = countdown(2, lambda: direct_sum(engine, "z", b["xy_sum"], b["last_x"], out_x))
-    last_z = countdown(2, lambda: direct_sum(engine, "y", b["zx_sum"], b["last_z"], out_z))
-    last_y = countdown(2, lambda: direct_sum(engine, "z", b["yx_sum"], b["last_y"], out_y))
+    last_x = countdown(2, lambda: direct_sum(engine, "z", "x", b["xy_sum"], b["last_x"], out))
+    last_z = countdown(2, lambda: direct_sum(engine, "y", "z", b["zx_sum"], b["last_z"], out))
+    last_y = countdown(2, lambda: direct_sum(engine, "z", "y", b["yx_sum"], b["last_y"], out))
     first_x = countdown(2, second_x)
 
     def start_sums(half):
@@ -465,12 +497,14 @@
                 ),
             )
 
-    a_part, b_part = inst // 2 // x_count, inst // 4 // z_count
-    a_from, b_from = inst // 4, 3 * inst // 4
-    c_part = inst // 8
+    c_part = inst // 32 * C_PARTS // 2
+    a_from = 2 * c_part
+    a_part, b_part = inst // 32 * A_PARTS // x_count, inst // 32 * B_PARTS // z_count
+    b_from = a_from + a_part * x_count
+    c_halves = (0, 1) if c_part else ()
     turn = itertools.count()
     complete = {
-        o: countdown(x_count + z_count + 3, lambda o=o: engine.work(LOGITS_COST, logits_of(o)))
+        o: countdown(x_count + z_count + 1 + len(c_halves), lambda o=o: engine.work(LOGITS_COST, logits_of(o)))
         for o in range(1, y_count)
     }
 
@@ -531,7 +565,7 @@
     engine.send("core", 1, rows, rows_all.at[pl.ds(stored, stored)], swapped)
     for o in range(1, y_count):
         engine.send("y", o, pos, p_all.at[place.y], complete[-o % y_count])
-    for half in (0, 1):
+    for half in c_halves:
         spread(
             engine, "y", half, from_feats(half * c_part, c_part),
             lambda p, half=half: cut(p, half * c_part, c_part), lambda o: complete[o](),
@@ -550,12 +584,14 @@
     scratch += [pltpu.SemaphoreType.DMA((n,)) for n in (3, copies, copies)]
     return pl.pallas_call(
         functools.partial(step_kernel, sizes, list(buffers)),
-        out_shape=[jax.ShapeDtypeStruct((8, inst), jnp.float32)]
-        + [jax.ShapeDtypeStruct((SHARES[c] * UNIT, BLK), jnp.float32) for c in "xzy"],
+        out_shape=[
+            jax.ShapeDtypeStruct((inst // BLK, BLK), jnp.float32),
+            jax.ShapeDtypeStruct((2 * UNIT, inst), jnp.bfloat16),
+        ],
         in_specs=[pl.BlockSpec(memory_space=pltpu.SMEM)] * 2
         + [pl.BlockSpec(memory_space=pl.ANY)] * 3
         + [pl.BlockSpec(memory_space=pltpu.VMEM)],
-        out_specs=[pl.BlockSpec(memory_space=pltpu.VMEM)] * 4,
+        out_specs=[pl.BlockSpec(memory_space=pltpu.VMEM)] * 2,
         scratch_shapes=scratch,
         compiler_params=pltpu.CompilerParams(
             collective_id=0, has_side_effects=True, vmem_limit_bytes=VMEM_LIMIT
@@ -587,15 +623,8 @@
     mask = jnp.sum(member, axis=3).astype(jnp.float32).transpose(0, 2, 1)
     mask = jnp.broadcast_to(mask[..., None], mask.shape + (BLK,)).reshape(y_count, CORES, inst)
 
-    loss, share_x, share_z, share_y = step(sizes, pick, cluster, feats, positives.T, weights, mask)
-    lanes = [
-        share_x[: 2 * UNIT],
-        jnp.concatenate([share_x[2 * UNIT :], share_z[:UNIT]]),
-        share_z[UNIT:],
-        share_y,
-    ]
-    grads = jnp.concatenate(lanes, axis=1).T
-    return loss[0], grads.astype(jnp.bfloat16)
+    loss, grads = step(sizes, pick, cluster, feats, positives.T, weights, mask)
+    return loss.reshape(-1), grads.T
 
 
 def solution(mesh, x_count=X_CHIPS):

time: 160 us -> 155 us (0.969)
  Pallas kernels: 150 us -> 145 us
  other arithmetic: 4.7 us -> 1.88 us
    pallas_call x1, Pallas kernels: 150 us -> 145 us  [step(): pl.pallas_call(functools.partial(step_kernel, sizes, list(buffers)), out_...]
    unnamed x0 -> x2, local copies, waits for them, and re-layouts: none -> 2.61 us
    another operation x3 -> x0, other arithmetic: 2.2 us -> none
where the time goes in v3:
time: 155 us; the launch traced here: 153 us
  Pallas kernels  145 us (94%)
  local copies, waits for them, and re-layouts  5.88 us (4%)
  other arithmetic  1.88 us (1%)
    pallas_call x1, Pallas kernels, step(): pl.pallas_call(functools.partial(step_kernel, sizes, list(buffers)), out_...  145 us

profile of v3, /device:TPU:6, one launch (start us, length us, event | category | flops | bytes accessed | tf_op | source)
XLA Modules:
  0.0 153.4 jit_solution(13152592854497902345)
XLA Ops:
  0.6 0.1 fusion.1
  0.7 0.1 iota_add_fusion
  0.8 0.1 add.49
  0.9 0.9 select_reduce_fusion
  1.8 0.1 mul.41
  1.9 0.9 reshape.57
  2.7 0.7 compare_reduce_fusion
  3.5 0.1 copy.16
  3.6 0.1 multiply_reduce_fusion
  3.7 0.7 copy.19.cluster
  4.3 0.1 copy.17
  4.4 0.7 copy.18.pick
  5.1 0.1 broadcast_in_dim.16
  5.2 0.7 reshape.58.mask
  5.8 144.9 %shard_map.68 = (f32[4,128]{1,0:T(4,128)}, bf16[32,512]{1,0:T(8,128)(2,1)}) custom-call(s32[8,2]{1,0:T(8,128)} %copy.18.pick, s32[8,2]{1,0:T(8,128)} %copy.19.cluster, bf16[512,1024]{1,0:T(8,128)(2,1)} %feats.1, s32[8,512]{1,0:T(8,128)} %bitcast.13, bf16[4,256,1024]{2,1,0:T(8,128)(2,1)} %rows.1, f32[8,2,512]{2,1,0:T(2,128)} %reshape.58.mask), custom_call_target="tpu_custom_call" | custom-call | tf_op jit(solution)/shard_map/pallas_call | solution.py:585
  150.8 1.2 copy.23
  152.0 1.4 copy.24
  (5 shorter events, 0.1 us)

commit v4 on v3

--- a/solution.py
+++ b/solution.py
@@ -21,8 +21,9 @@
 LINK_RATE = 51e3
 LINK_DELAY = 2.5
 ISSUE = 0.1
-LOGITS_COST = 1.5
-GRADS_COST = 1.2
+HITS_COST = 0.7
+LOGITS_COST = 1.0
+GRADS_COST = 0.8
 
 
 class Place:
@@ -190,7 +191,7 @@
         step(sign, length, 0)
 
 
-def direct_sum(engine, axis, first, total, slots, out):
+def direct_sum(engine, axis, put, total, slots):
     place = engine.place
     n = place.count[axis]
 
@@ -198,8 +199,7 @@
         value = total[place.at(axis, 0)]
         for o in range(1, n):
             value = value + slots[o - 1]
-        for place_in, rows_in, lanes_in in spots(first):
-            out[rows_in, lanes_in] = value[place_in].astype(out.dtype)
+        put(value)
 
     landed = countdown(n - 1, lambda: engine.work(0.2, finish))
     for o in range(1, n):
@@ -272,12 +272,14 @@
         "g_z": ((y, z, x, rows["z"], BLK), bf),
         "g_y": ((y, z, x, rows["y"], BLK), bf),
         "x_sum": ((y, z, rows["x"], BLK), f4),
-        "xy_sum": ((z, rows["x"], BLK), f4),
+        "xy_sum": ((z, rows["x"] // 2, BLK), f4),
+        "xz_sum": ((y, rows["x"] // 2, BLK), f4),
         "z_sum": ((y, x, rows["z"], BLK), f4),
         "zx_sum": ((y, rows["z"], BLK), f4),
         "y_sum": ((z, x, rows["y"], BLK), f4),
         "yx_sum": ((z, rows["y"], BLK), f4),
-        "last_x": ((z - 1, rows["x"], BLK), f4),
+        "last_xy": ((z - 1, rows["x"] // 2, BLK), f4),
+        "last_xz": ((y - 1, rows["x"] // 2, BLK), f4),
         "last_z": ((y - 1, rows["z"], BLK), f4),
         "last_y": ((z - 1, rows["y"], BLK), f4),
     }
@@ -285,11 +287,12 @@
         "x1": ("x", (y // 2, z, rows["x"], BLK), bf),
         "z1": ("z", (y // 2, x, rows["z"], BLK), bf),
         "y1": ("y", (z // 2, x, rows["y"], BLK), bf),
-        "x2": ("y", (z // 2, rows["x"], BLK), f4),
+        "xy2": ("y", (z // 2, rows["x"] // 2, BLK), f4),
+        "xz2": ("z", (y // 2, rows["x"] // 2, BLK), f4),
         "z2": ("x", (y // 2, rows["z"], BLK), f4),
         "y2": ("x", (z // 2, rows["y"], BLK), f4),
     }
-    copies = 1 + 2 * (z - 1) + (y - 1)
+    copies = 1 + 2 * (z - 1) + 2 * (y - 1)
     for name, (axis, shape, dtype) in rings.items():
         for sign in (1, -1):
             for half in (0, 1):
@@ -300,7 +303,7 @@
     return buffers, copies
 
 
-def step_kernel(sizes, names, pick, cluster, feats, pos, rows, mask, loss, out, *scratch):
+def step_kernel(sizes, names, info, feats, pos, rows, lse_out, found_out, out, *scratch):
     y_count, z_count, x_count = sizes
     place = Place(*sizes)
     b = dict(zip(names, scratch))
@@ -330,6 +333,28 @@
         + [place.device("core", 1)]
     )
     engine = Engine(place, send_sem, recv_sem)
+    fields = 2 + blocks
+
+    def pick(d, s):
+        return s * stored + info[d, s * fields]
+
+    def hits_of(offset, done):
+        def run():
+            d = place.at("y", offset)
+
+            def one(s, carry):
+                shape = (size, inst)
+                label = info[d, s * fields + 1] * size + lax.broadcasted_iota(jnp.int32, shape, 0)
+                hit = p_all[d, 0:1, :] == label
+                for p in range(1, pos_count):
+                    hit = hit | (p_all[d, p : p + 1, :] == label)
+                hits[d, s] = jnp.where(hit, 1.0 / pos_count, 0.0).astype(jnp.bfloat16)
+                return carry
+
+            lax.fori_loop(0, CORES, one, 0)
+            done()
+
+        return run
 
     def logits_of(offset):
         def run():
@@ -337,22 +362,20 @@
 
             def one(s, carry):
                 logits = lax.dot_general(
-                    rows_all[s * stored + pick[d, s]],
+                    rows_all[pick(d, s)],
                     f_all[d],
                     (((1,), (1,)), ((), ())),
                     preferred_element_type=jnp.float32,
                 )
-                label = cluster[d, s] * size + lax.broadcasted_iota(jnp.int32, logits.shape, 0)
-                hit = p_all[d, 0:1, :] == label
-                for p in range(1, pos_count):
-                    hit = hit | (p_all[d, p : p + 1, :] == label)
-                hits[d, s] = jnp.where(hit, 1.0 / pos_count, 0.0).astype(jnp.bfloat16)
-                valid = jnp.where(mask[d, pl.ds(s, 1), :] > 0, logits, NEG_FILL)
+                member = jnp.concatenate(
+                    [jnp.full((1, BLK), info[d, s * fields + 2 + i]) for i in range(blocks)], axis=1
+                )
+                valid = jnp.where(member > 0, logits, NEG_FILL)
                 high = jnp.max(valid, axis=0, keepdims=True)
                 power = jnp.exp(valid - high)
                 kept[d, s] = power
                 total = jnp.sum(power, axis=0, keepdims=True)
-                found = jnp.sum(jnp.where(hit, logits, 0.0), axis=0, keepdims=True)
+                found = jnp.sum(hits[d, s].astype(jnp.float32) * logits, axis=0, keepdims=True)
                 write(peaks.at[d, s], folded(high) + folded(total) + folded(found))
                 return carry
 
@@ -391,7 +414,8 @@
         landed = countdown(y_count - 1, queue_grads)
         for o in range(1, y_count):
             engine.send("y", o, lse_mine, lse_all.at[place.y], landed)
-        loss[...] = lse - found / pos_count
+        lse_out[...] = lse
+        found_out[...] = found
         lse_all[place.y] = lse_mine[...]
 
     stat_landed = countdown(y_count, lambda: engine.work(0.2, over_y))
@@ -406,7 +430,7 @@
                     scale = unfolded(jnp.exp(peaks[d, s][:blocks] - lse))
                     dlogit = kept[d, s] * scale - hits[d, s].astype(jnp.float32)
                     term = jnp.dot(
-                        turned[s * stored + pick[d, s]],
+                        turned[pick(d, s)],
                         dlogit.astype(jnp.bfloat16),
                         preferred_element_type=jnp.float32,
                     )
@@ -432,22 +456,51 @@
     def part(half, count):
         return pl.ds(half * count, count)
 
-    def second_x():
+    def put(axis, start):
+        def run(value):
+            stop = start + value.shape[0]
+            for place_in, rows_in, lanes_in in spots(axis):
+                low, high = max(place_in.start, start), min(place_in.stop, stop)
+                if low < high:
+                    first = rows_in.start + low - place_in.start
+                    out[first : first + high - low, lanes_in] = value[low - start : high - start]
+
+        return run
+
+    def put_x(which):
+        return put("x", which * x_part)
+
+    x_part = SHARES["x"] * UNIT // 2
+
+    def second_xy():
         for half in (0, 1):
             ring_sum(
                 engine,
                 "y",
                 half,
-                lambda dest, half=half: b["x_sum"].at[dest, part(half, z_half)],
-                slots("x2"),
+                lambda dest, half=half: b["x_sum"].at[dest, part(half, z_half), :x_part],
+                slots("xy2"),
                 b["xy_sum"].at[part(half, z_half)],
-                last_x,
+                last_xy,
             )
 
-    last_x = countdown(2, lambda: direct_sum(engine, "z", "x", b["xy_sum"], b["last_x"], out))
-    last_z = countdown(2, lambda: direct_sum(engine, "y", "z", b["zx_sum"], b["last_z"], out))
-    last_y = countdown(2, lambda: direct_sum(engine, "z", "y", b["yx_sum"], b["last_y"], out))
-    first_x = countdown(2, second_x)
+    def second_xz(half):
+        ring_sum(
+            engine,
+            "z",
+            half,
+            lambda dest: b["x_sum"].at[part(half, y_half), dest, x_part:],
+            slots("xz2"),
+            b["xz_sum"].at[part(half, y_half)],
+            last_xz,
+        )
+        first_x()
+
+    last_xy = countdown(2, lambda: direct_sum(engine, "z", put_x(0), b["xy_sum"], b["last_xy"]))
+    last_xz = countdown(2, lambda: direct_sum(engine, "y", put_x(1), b["xz_sum"], b["last_xz"]))
+    last_z = countdown(2, lambda: direct_sum(engine, "y", put("z", 0), b["zx_sum"], b["last_z"]))
+    last_y = countdown(2, lambda: direct_sum(engine, "z", put("y", 0), b["yx_sum"], b["last_y"]))
+    first_x = countdown(2, second_xy)
 
     def start_sums(half):
         ring_sum(
@@ -474,7 +527,7 @@
             lambda dest: b["g_x"].at[part(half, y_half), :, dest],
             slots("x1"),
             b["x_sum"].at[part(half, y_half)],
-            first_x,
+            lambda: second_xz(half),
         )
         if half == 0:
             return
@@ -502,11 +555,16 @@
     a_part, b_part = inst // 32 * A_PARTS // x_count, inst // 32 * B_PARTS // z_count
     b_from = a_from + a_part * x_count
     c_halves = (0, 1) if c_part else ()
-    turn = itertools.count()
+    turn_a, turn_b = itertools.count(), itertools.count()
     complete = {
         o: countdown(x_count + z_count + 1 + len(c_halves), lambda o=o: engine.work(LOGITS_COST, logits_of(o)))
         for o in range(1, y_count)
     }
+
+    complete[0] = countdown(2, lambda: engine.work(LOGITS_COST, logits_of(0)))
+
+    def hits_next(o):
+        return lambda: engine.work(HITS_COST, hits_of(o, complete[o]))
 
     def cut(origin, start, count):
         return f_all.at[origin, pl.ds(pl.multiple_of(start, 16), count)]
@@ -517,7 +575,7 @@
         spread(
             engine,
             "x",
-            next(turn) % 2,
+            next(turn_a) % 2,
             lambda: cut(origin, a_from + place.x * a_part, a_part),
             lambda p: cut(origin, a_from + p * a_part, a_part),
             lambda _: complete[o](),
@@ -529,7 +587,7 @@
         spread(
             engine,
             "z",
-            next(turn) % 2,
+            next(turn_b) % 2,
             lambda: cut(origin, b_from + place.z * b_part, b_part),
             lambda p: cut(origin, b_from + p * b_part, b_part),
             lambda _: complete[o](),
@@ -549,22 +607,22 @@
         return run
 
     def swapped():
-        engine.work(LOGITS_COST, logits_of(0))
+        complete[0]()
         engine.work(3.0, turn_rows(stored))
 
+    start = b_from + place.z * b_part
+    spread(
+        engine, "y", 1, from_feats(start, b_part),
+        lambda p, start=start: cut(p, start, b_part), b_landed,
+    )
     start = a_from + place.x * a_part
     spread(
         engine, "y", 0, from_feats(start, a_part),
         lambda p, start=start: cut(p, start, a_part), a_landed,
     )
-    start = b_from + place.z * b_part
-    spread(
-        engine, "y", 1, from_feats(start, b_part),
-        lambda p, start=start: cut(p, start, b_part), b_landed,
-    )
     engine.send("core", 1, rows, rows_all.at[pl.ds(stored, stored)], swapped)
     for o in range(1, y_count):
-        engine.send("y", o, pos, p_all.at[place.y], complete[-o % y_count])
+        engine.send("y", o, pos, p_all.at[place.y], hits_next(-o % y_count))
     for half in c_halves:
         spread(
             engine, "y", half, from_feats(half * c_part, c_part),
@@ -572,11 +630,12 @@
         )
     for copy in locals_:
         copy.wait()
+    hits_next(0)()
     engine.work(3.0, turn_rows(0))
     engine.run()
 
 
-def step(sizes, pick, cluster, feats, pos, rows, mask):
+def step(sizes, info, feats, pos, rows):
     inst, width = feats.shape
     stored, size, _ = rows.shape
     buffers, copies = plan(sizes, inst, width, size, stored, pos.shape[0])
@@ -586,17 +645,16 @@
         functools.partial(step_kernel, sizes, list(buffers)),
         out_shape=[
             jax.ShapeDtypeStruct((inst // BLK, BLK), jnp.float32),
-            jax.ShapeDtypeStruct((2 * UNIT, inst), jnp.bfloat16),
+            jax.ShapeDtypeStruct((inst // BLK, BLK), jnp.float32),
+            jax.ShapeDtypeStruct((2 * UNIT, inst), jnp.float32),
         ],
-        in_specs=[pl.BlockSpec(memory_space=pltpu.SMEM)] * 2
-        + [pl.BlockSpec(memory_space=pl.ANY)] * 3
-        + [pl.BlockSpec(memory_space=pltpu.VMEM)],
-        out_specs=[pl.BlockSpec(memory_space=pltpu.VMEM)] * 2,
+        in_specs=[pl.BlockSpec(memory_space=pltpu.SMEM)] + [pl.BlockSpec(memory_space=pl.ANY)] * 3,
+        out_specs=[pl.BlockSpec(memory_space=pltpu.VMEM)] * 3,
         scratch_shapes=scratch,
         compiler_params=pltpu.CompilerParams(
             collective_id=0, has_side_effects=True, vmem_limit_bytes=VMEM_LIMIT
         ),
-    )(pick, cluster, feats, pos, rows, mask)
+    )(info, feats, pos, rows)
 
 
 def shards(x_count, feats, weights, shortlist, slot_of, positives):
@@ -613,18 +671,16 @@
     slots = (pair[:, None] * stored + jnp.arange(stored, dtype=jnp.int32)).reshape(-1)
     ids = jnp.arange(slot_of.shape[0], dtype=jnp.int32)
     clusters = jnp.sum(jnp.where(slots[:, None] == slot_of[None, :], ids[None, :], 0), axis=1)
-    lists = shortlist.reshape(y_count, CORES, block_count, -1)
-    lists = lax.dynamic_index_in_dim(lists, core, 1, keepdims=False)
-    member = jnp.any(lists[:, :, None, :] == clusters[None, None, :, None], axis=3)
-    member = member.reshape(y_count, block_count, CORES, stored).astype(jnp.int32)
+    member = jnp.any(shortlist[:, None, :] == clusters[None, :, None], axis=2)
+    member = member.reshape(y_count, CORES, block_count, CORES, stored)
+    member = lax.dynamic_index_in_dim(member, core, 1, keepdims=False).astype(jnp.int32)
     chosen = jnp.sum(member[:, :half_blocks], axis=1)
     pick = jnp.sum(chosen * jnp.arange(stored, dtype=jnp.int32), axis=2)
     cluster = jnp.sum(chosen * clusters.reshape(1, CORES, stored), axis=2)
-    mask = jnp.sum(member, axis=3).astype(jnp.float32).transpose(0, 2, 1)
-    mask = jnp.broadcast_to(mask[..., None], mask.shape + (BLK,)).reshape(y_count, CORES, inst)
-
-    loss, grads = step(sizes, pick, cluster, feats, positives.T, weights, mask)
-    return loss.reshape(-1), grads.T
+    blocks = jnp.sum(member, axis=3).transpose(0, 2, 1)
+    info = jnp.concatenate([pick[..., None], cluster[..., None], blocks], axis=2)
+    lse, found, grads = step(sizes, info.reshape(y_count, -1), feats, positives.T, weights)
+    return (lse - found).reshape(-1), grads.astype(jnp.bfloat16).T
 
 
 def solution(mesh, x_count=X_CHIPS):

time: 155 us -> 150 us (0.968)
  Pallas kernels: 145 us -> 140 us
  local copies, waits for them, and re-layouts: 5.88 us -> 1.24 us
  other arithmetic: 1.88 us -> 6.28 us
    pallas_call x1, Pallas kernels: 145 us -> 140 us  [step(): pl.pallas_call(functools.partial(step_kernel, sizes, list(buffers)), out_...]
    unnamed x2 -> x0, local copies, waits for them, and re-layouts: 2.61 us -> none
where the time goes in v4:
time: 150 us; the launch traced here: 148 us
  Pallas kernels  140 us (93%)
  other arithmetic  6.28 us (4%)
    pallas_call x1, Pallas kernels, step(): pl.pallas_call(functools.partial(step_kernel, sizes, list(buffers)), out_...  140 us

profile of v4, /device:TPU:6, one launch (start us, length us, event | category | flops | bytes accessed | tf_op | source)
XLA Modules:
  0.0 148.4 jit_solution(4283765536489564752)
XLA Ops:
  0.6 0.1 fusion.1
  0.7 0.1 iota_add_fusion
  0.8 0.1 add.48
  0.9 0.9 select_reduce_fusion
  1.8 0.1 mul.41
  1.9 2.1 %compare_reduce_fusion = pred[64,8]{1,0:T(8,128)(4,1)S(1)} fusion(s32[64,256]{1,0:T(8,128)} %param.7, s32[8]{0:T(128)S(1)} %select_reduce_fusion), kind=kLoop, calls=%fused_computation | loop fusion | flops 261632 | bytes 66080 | tf_op jit(solution)/shard_map/reduce_or | solution.py:674
  3.9 0.1 copy.14
  4.0 0.1 reshape.53
  4.2 0.1 fusion.2
  4.2 0.2 slice_reduce_fusion
  4.5 0.1 multiply_reduce_fusion.1
  4.5 0.1 copy.16
  4.6 0.1 copy.15
  4.7 0.1 pad_add_fusion
  4.8 0.7 reshape.54.info
  5.5 140.2 %shard_map.68 = (f32[4,128]{1,0:T(4,128)}, f32[4,128]{1,0:T(4,128)}, f32[32,512]{1,0:T(8,128)}) custom-call(s32[8,12]{1,0:T(8,128)} %reshape.54.info, bf16[512,1024]{1,0:T(8,128)(2,1)} %feats.1, s32[8,512]{1,0:T(8,128)} %bitcast.15, bf16[4,256,1024]{2,1,0:T(8,128)(2,1)} %rows.1), custom_call_target="tpu_custom_call" | custom-call | tf_op jit(solution)/shard_map/pallas_call | solution.py:644
  145.7 1.3 subtract_bitcast_fusion
  147.0 1.5 convert_bitcast_fusion
  (1 shorter events, 0.0 us)

commit v5 on v4

--- a/solution.py
+++ b/solution.py
@@ -17,7 +17,6 @@
 NEG_FILL = -1e30
 MESH = pl.DeviceIdType.MESH
 A_PARTS, B_PARTS, C_PARTS = 16, 16, 0
-FAR = {"y": 1, "z": 1, "x": 1}
 LINK_RATE = 51e3
 LINK_DELAY = 2.5
 ISSUE = 0.1
@@ -127,19 +126,14 @@
     place = engine.place
     n = place.count[axis]
 
-    far = FAR[axis]
-
     def pass_on(sign, k):
-        origin = place.at(axis, -sign * k)
-        src = target(origin) if k else source()
-        for hops in range(1, min(far, reach(n, sign, half) - k) + 1):
-            engine.send(
-                axis, sign * hops, src, target(origin), lambda hops=hops: landed(sign, k + hops)
-            )
+        if k < reach(n, sign, half):
+            origin = place.at(axis, -sign * k)
+            src = target(origin) if k else source()
+            engine.send(axis, sign, src, target(origin), lambda: landed(sign, k + 1))
 
     def landed(sign, k):
-        if k % far == 0:
-            pass_on(sign, k)
+        pass_on(sign, k)
         arrived(-sign * k % n)
 
     for sign in (1, -1):
@@ -189,6 +183,56 @@
 
     for sign, length in chains:
         step(sign, length, 0)
+
+
+def hub_sum(engine, axis, half, own, slots, total, done):
+    place = engine.place
+    n = place.count[axis]
+    chains = [(sign, reach(n, sign, half)) for sign in (1, -1) if reach(n, sign, half) > 0]
+    near, hub, third, fourth = range(4)
+
+    def finish():
+        first = own(place.at(axis, 0))
+        parts = [
+            slots[sign, half].at[k] for sign, length in chains for k in range(min(length, 2))
+        ]
+
+        def one(i, carry):
+            value = first[i]
+            for part in parts:
+                value = value + part[i]
+            total[i] = value
+            return carry
+
+        lax.fori_loop(0, total.shape[0], one, 0)
+        done()
+
+    landed = countdown(
+        sum(min(length, 2) for _, length in chains), lambda: engine.work(0.3, finish)
+    )
+
+    def start(sign, length):
+        inbox = slots[sign, half]
+
+        def relay():
+            ref = own(place.at(axis, 2 * sign))
+            for k in range(fourth, hub, -1):
+                if k < length:
+                    add_into(inbox.at[k], ref)
+                    ref = inbox.at[k]
+                    engine.now += 0.2
+            engine.send(axis, 2 * sign, ref, inbox.at[hub], landed)
+
+        collected = countdown(length - 2, relay) if length > 2 else None
+        for k in range(fourth, hub, -1):
+            if k < length:
+                engine.send(axis, (k - 1) * sign, own(place.at(axis, (k + 1) * sign)), inbox.at[k], collected)
+        if length == 2:
+            relay()
+        engine.send(axis, sign, own(place.at(axis, sign)), inbox.at[near], landed)
+
+    for sign, length in chains:
+        start(sign, length)
 
 
 def direct_sum(engine, axis, put, total, slots):
@@ -474,7 +518,7 @@
 
     def second_xy():
         for half in (0, 1):
-            ring_sum(
+            hub_sum(
                 engine,
                 "y",
                 half,
@@ -485,7 +529,7 @@
             )
 
     def second_xz(half):
-        ring_sum(
+        hub_sum(
             engine,
             "z",
             half,
@@ -503,35 +547,7 @@
     first_x = countdown(2, second_xy)
 
     def start_sums(half):
-        ring_sum(
-            engine,
-            "z",
-            half,
-            lambda dest: b["g_z"].at[part(half, y_half), dest],
-            slots("z1"),
-            b["z_sum"].at[part(half, y_half)],
-            lambda: ring_sum(
-                engine,
-                "x",
-                half,
-                lambda dest: b["z_sum"].at[part(half, y_half), dest],
-                slots("z2"),
-                b["zx_sum"].at[part(half, y_half)],
-                last_z,
-            ),
-        )
-        ring_sum(
-            engine,
-            "x",
-            half,
-            lambda dest: b["g_x"].at[part(half, y_half), :, dest],
-            slots("x1"),
-            b["x_sum"].at[part(half, y_half)],
-            lambda: second_xz(half),
-        )
-        if half == 0:
-            return
-        for zh in (0, 1):
+        for zh in (0, 1) if half else ():
             ring_sum(
                 engine,
                 "y",
@@ -549,6 +565,32 @@
                     last_y,
                 ),
             )
+        ring_sum(
+            engine,
+            "z",
+            half,
+            lambda dest: b["g_z"].at[part(half, y_half), dest],
+            slots("z1"),
+            b["z_sum"].at[part(half, y_half)],
+            lambda: ring_sum(
+                engine,
+                "x",
+                half,
+                lambda dest: b["z_sum"].at[part(half, y_half), dest],
+                slots("z2"),
+                b["zx_sum"].at[part(half, y_half)],
+                last_z,
+            ),
+        )
+        ring_sum(
+            engine,
+            "x",
+            half,
+            lambda dest: b["g_x"].at[part(half, y_half), :, dest],
+            slots("x1"),
+            b["x_sum"].at[part(half, y_half)],
+            lambda: second_xz(half),
+        )
 
     c_part = inst // 32 * C_PARTS // 2
     a_from = 2 * c_part
@@ -671,9 +713,10 @@
     slots = (pair[:, None] * stored + jnp.arange(stored, dtype=jnp.int32)).reshape(-1)
     ids = jnp.arange(slot_of.shape[0], dtype=jnp.int32)
     clusters = jnp.sum(jnp.where(slots[:, None] == slot_of[None, :], ids[None, :], 0), axis=1)
-    member = jnp.any(shortlist[:, None, :] == clusters[None, :, None], axis=2)
-    member = member.reshape(y_count, CORES, block_count, CORES, stored)
-    member = lax.dynamic_index_in_dim(member, core, 1, keepdims=False).astype(jnp.int32)
+    lists = shortlist.reshape(y_count, CORES * block_count, -1)
+    lists = lax.dynamic_slice_in_dim(lists, core * block_count, block_count, axis=1)
+    member = jnp.any(lists[:, :, None, :] == clusters[None, None, :, None], axis=3)
+    member = member.reshape(y_count, block_count, CORES, stored).astype(jnp.int32)
     chosen = jnp.sum(member[:, :half_blocks], axis=1)
     pick = jnp.sum(chosen * jnp.arange(stored, dtype=jnp.int32), axis=2)
     cluster = jnp.sum(chosen * clusters.reshape(1, CORES, stored), axis=2)

time: 150 us -> 148 us (0.987); the launches traced: 148 us -> 148 us
  other arithmetic: 6.28 us -> 4.59 us
where the time goes in v5:
time: 148 us
  Pallas kernels  141 us (95%)
  other arithmetic  4.59 us (3%)
  local copies, waits for them, and re-layouts  1.76 us (1%)
    pallas_call x1, Pallas kernels, step(): pl.pallas_call(functools.partial(step_kernel, sizes, list(buffers)), out_...  141 us

profile of v5, /device:TPU:6, one launch (start us, length us, event | category | flops | bytes accessed | tf_op | source)
XLA Modules:
  0.0 148.0 jit_solution(4322181241939396951)
XLA Ops:
  0.6 0.0 copy-start
  0.7 0.1 fusion.1
  0.7 0.7 copy-done
  1.5 0.1 iota_add_fusion
  1.5 0.1 add.48
  1.6 0.9 select_reduce_fusion
  2.5 0.1 mul.45
  2.6 0.7 compare_reduce_fusion
  3.3 0.1 copy.15
  3.5 0.1 multiply_reduce_fusion.1
  3.6 0.1 copy.16
  3.6 0.7 reshape.56.info
  4.3 140.9 %shard_map.68 = (f32[4,128]{1,0:T(4,128)}, f32[4,128]{1,0:T(4,128)}, f32[32,512]{1,0:T(8,128)}) custom-call(s32[8,12]{1,0:T(8,128)} %reshape.56.info, bf16[512,1024]{1,0:T(8,128)(2,1)} %feats.1, s32[8,512]{1,0:T(8,128)} %bitcast.15, bf16[4,256,1024]{2,1,0:T(8,128)(2,1)} %rows.1), custom_call_target="tpu_custom_call" | custom-call | tf_op jit(solution)/shard_map/pallas_call | solution.py:686
  145.3 1.3 subtract_bitcast_fusion
  146.5 1.5 convert_bitcast_fusion
  (5 shorter events, 0.1 us)
Async XLA Ops:
  0.6 0.8 copy-start

commit v6 on v5

--- a/solution.py
+++ b/solution.py
@@ -21,6 +21,7 @@
 LINK_DELAY = 2.5
 ISSUE = 0.1
 HITS_COST = 0.7
+TURN_COST = 0.7
 LOGITS_COST = 1.0
 GRADS_COST = 0.8
 
@@ -89,13 +90,13 @@
         )
         self.now += ISSUE
 
-    def work(self, cost, run):
-        self.ready.append((cost, run))
+    def work(self, cost, run, later=False):
+        heapq.heappush(self.ready, (later, next(self.order), cost, run))
 
     def run(self):
         while self.heap or self.ready:
             if self.ready and (not self.heap or self.heap[0][0] > self.now):
-                cost, run = self.ready.pop(0)
+                _, _, cost, run = heapq.heappop(self.ready)
                 self.now += cost
                 run()
                 continue
@@ -433,7 +434,15 @@
 
         return run
 
+    def turn_rows(i):
+        def run():
+            turned[i] = rows_all[i].T
+
+        return run
+
     def over_y():
+        for i in range(CORES * stored):
+            engine.work(TURN_COST, turn_rows(i), later=True)
         held[0] = jnp.zeros_like(held[0])
         write(
             held.at[0],
@@ -492,7 +501,7 @@
 
     def queue_grads():
         for half in (0, 1):
-            engine.work(y_half * GRADS_COST, grads_of(half))
+            engine.work(y_half * GRADS_COST, grads_of(half), later=True)
 
     def slots(name):
         return {(sign, half): b[name, sign, half] for sign in (1, -1) for half in (0, 1)}
@@ -638,19 +647,8 @@
     def from_feats(start, count):
         return lambda: feats.at[pl.ds(pl.multiple_of(start, 16), count)]
 
-    def turn_rows(base):
-        def run():
-            def one(i, carry):
-                turned[base + i] = rows_all[base + i].T
-                return carry
-
-            lax.fori_loop(0, stored, one, 0)
-
-        return run
-
     def swapped():
         complete[0]()
-        engine.work(3.0, turn_rows(stored))
 
     start = b_from + place.z * b_part
     spread(
@@ -673,7 +671,6 @@
     for copy in locals_:
         copy.wait()
     hits_next(0)()
-    engine.work(3.0, turn_rows(0))
     engine.run()
 
 

time: 148 us -> 146 us (0.986)
  Pallas kernels: 141 us -> 138 us
    pallas_call x1, Pallas kernels: 141 us -> 138 us  [step(): pl.pallas_call(functools.partial(step_kernel, sizes, list(buffers)), out_...]
where the time goes in v6:
time: 146 us; the launch traced here: 145 us
  Pallas kernels  138 us (95%)
  other arithmetic  4.59 us (3%)
  local copies, waits for them, and re-layouts  1.76 us (1%)
    pallas_call x1, Pallas kernels, step(): pl.pallas_call(functools.partial(step_kernel, sizes, list(buffers)), out_...  138 us

profile of v6, /device:TPU:6, one launch (start us, length us, event | category | flops | bytes accessed | tf_op | source)
XLA Modules:
  0.0 144.7 jit_solution(16400035075071021464)
XLA Ops:
  0.6 0.0 copy-start
  0.7 0.1 fusion.1
  0.7 0.7 copy-done
  1.5 0.1 iota_add_fusion
  1.5 0.1 add.48
  1.6 0.9 select_reduce_fusion
  2.5 0.1 mul.45
  2.6 0.7 compare_reduce_fusion
  3.3 0.1 copy.15
  3.5 0.1 multiply_reduce_fusion.1
  3.6 0.1 copy.16
  3.6 0.7 reshape.56.info
  4.3 137.7 %shard_map.68 = (f32[4,128]{1,0:T(4,128)}, f32[4,128]{1,0:T(4,128)}, f32[32,512]{1,0:T(8,128)}) custom-call(s32[8,12]{1,0:T(8,128)} %reshape.56.info, bf16[512,1024]{1,0:T(8,128)(2,1)} %feats.1, s32[8,512]{1,0:T(8,128)} %bitcast.15, bf16[4,256,1024]{2,1,0:T(8,128)(2,1)} %rows.1), custom_call_target="tpu_custom_call" | custom-call | tf_op jit(solution)/shard_map/pallas_call | solution.py:683
  142.0 1.3 subtract_bitcast_fusion
  143.2 1.5 %convert_bitcast_fusion = bf16[512,32]{0,1:T(8,128)(2,1)} fusion(f32[32,512]{1,0:T(8,128)} %get-tuple-element.7), kind=kLoop, calls=%fused_computation.2 | loop fusion | flops 16384 | bytes 98304 | tf_op jit(solution)/shard_map/transpose | solution.py:723
  (5 shorter events, 0.1 us)
Async XLA Ops:
  0.6 0.8 copy-start

commit v7 on v6

--- a/solution.py
+++ b/solution.py
@@ -19,10 +19,10 @@
 A_PARTS, B_PARTS, C_PARTS = 16, 16, 0
 LINK_RATE = 51e3
 LINK_DELAY = 2.5
-ISSUE = 0.1
-HITS_COST = 0.7
+ISSUE = 0.04
+HITS_COST = 0.35
 TURN_COST = 0.7
-LOGITS_COST = 1.0
+LOGITS_COST = 0.5
 GRADS_COST = 0.8
 
 
@@ -383,48 +383,47 @@
     def pick(d, s):
         return s * stored + info[d, s * fields]
 
-    def hits_of(offset, done):
+    def hits_of(offset, s, done):
         def run():
             d = place.at("y", offset)
 
-            def one(s, carry):
-                shape = (size, inst)
-                label = info[d, s * fields + 1] * size + lax.broadcasted_iota(jnp.int32, shape, 0)
-                hit = p_all[d, 0:1, :] == label
-                for p in range(1, pos_count):
-                    hit = hit | (p_all[d, p : p + 1, :] == label)
-                hits[d, s] = jnp.where(hit, 1.0 / pos_count, 0.0).astype(jnp.bfloat16)
-                return carry
-
-            lax.fori_loop(0, CORES, one, 0)
+            shape = (size, inst)
+            label = info[d, s * fields + 1] * size + lax.broadcasted_iota(jnp.int32, shape, 0)
+            hit = p_all[d, 0:1, :] == label
+            for p in range(1, pos_count):
+                hit = hit | (p_all[d, p : p + 1, :] == label)
+            hits[d, s] = jnp.where(hit, 1.0 / pos_count, 0.0).astype(jnp.bfloat16)
             done()
 
         return run
 
-    def logits_of(offset):
+    def logits_of(offset, s, done):
         def run():
             d = place.at("y", offset)
 
-            def one(s, carry):
-                logits = lax.dot_general(
-                    rows_all[pick(d, s)],
-                    f_all[d],
-                    (((1,), (1,)), ((), ())),
-                    preferred_element_type=jnp.float32,
-                )
-                member = jnp.concatenate(
-                    [jnp.full((1, BLK), info[d, s * fields + 2 + i]) for i in range(blocks)], axis=1
-                )
-                valid = jnp.where(member > 0, logits, NEG_FILL)
-                high = jnp.max(valid, axis=0, keepdims=True)
-                power = jnp.exp(valid - high)
-                kept[d, s] = power
-                total = jnp.sum(power, axis=0, keepdims=True)
-                found = jnp.sum(hits[d, s].astype(jnp.float32) * logits, axis=0, keepdims=True)
-                write(peaks.at[d, s], folded(high) + folded(total) + folded(found))
-                return carry
-
-            lax.fori_loop(0, CORES, one, 0)
+            logits = lax.dot_general(
+                rows_all[pick(d, s)],
+                f_all[d],
+                (((1,), (1,)), ((), ())),
+                preferred_element_type=jnp.float32,
+            )
+            member = jnp.concatenate(
+                [jnp.full((1, BLK), info[d, s * fields + 2 + i]) for i in range(blocks)], axis=1
+            )
+            valid = jnp.where(member > 0, logits, NEG_FILL)
+            high = jnp.max(valid, axis=0, keepdims=True)
+            power = jnp.exp(valid - high)
+            kept[d, s] = power
+            total = jnp.sum(power, axis=0, keepdims=True)
+            found = jnp.sum(hits[d, s].astype(jnp.float32) * logits, axis=0, keepdims=True)
+            write(peaks.at[d, s], folded(high) + folded(total) + folded(found))
+            done()
+
+        return run
+
+    def stats_of(offset):
+        def run():
+            d = place.at("y", offset)
             stats[d] = jnp.zeros_like(stats[d])
             write(stats.at[d], merge([peaks[d, s] for s in range(CORES)], blocks))
             if offset % y_count:
@@ -606,16 +605,25 @@
     a_part, b_part = inst // 32 * A_PARTS // x_count, inst // 32 * B_PARTS // z_count
     b_from = a_from + a_part * x_count
     c_halves = (0, 1) if c_part else ()
+    def queue_logits(o):
+        landed = countdown(CORES, stats_of(o))
+        for s in range(CORES):
+            engine.work(LOGITS_COST, logits_of(o, s, landed))
+
     turn_a, turn_b = itertools.count(), itertools.count()
     complete = {
-        o: countdown(x_count + z_count + 1 + len(c_halves), lambda o=o: engine.work(LOGITS_COST, logits_of(o)))
+        o: countdown(x_count + z_count + CORES + len(c_halves), lambda o=o: queue_logits(o))
         for o in range(1, y_count)
     }
 
-    complete[0] = countdown(2, lambda: engine.work(LOGITS_COST, logits_of(0)))
+    complete[0] = countdown(1 + CORES, lambda: queue_logits(0))
 
     def hits_next(o):
-        return lambda: engine.work(HITS_COST, hits_of(o, complete[o]))
+        def run():
+            for s in range(CORES):
+                engine.work(HITS_COST, hits_of(o, s, complete[o]))
+
+        return run
 
     def cut(origin, start, count):
         return f_all.at[origin, pl.ds(pl.multiple_of(start, 16), count)]

time: 146 us -> 147 us (level)
    pallas_call x1, Pallas kernels: 138 us -> 139 us  [step(): pl.pallas_call(functools.partial(step_kernel, sizes, list(buffers)), out_...]
where the time goes in v7:
time: 147 us; the launch traced here: 146 us
  Pallas kernels  139 us (95%)
  other arithmetic  4.59 us (3%)
  local copies, waits for them, and re-layouts  1.76 us (1%)
    pallas_call x1, Pallas kernels, step(): pl.pallas_call(functools.partial(step_kernel, sizes, list(buffers)), out_...  139 us

profile of v7, /device:TPU:6, one launch (start us, length us, event | category | flops | bytes accessed | tf_op | source)
XLA Modules:
  0.0 146.3 jit_solution(11455791152141201740)
XLA Ops:
  0.6 0.0 copy-start
  0.7 0.1 fusion.1
  0.7 0.7 copy-done
  1.5 0.1 iota_add_fusion
  1.5 0.1 add.48
  1.6 0.9 select_reduce_fusion
  2.5 0.1 mul.45
  2.6 0.7 compare_reduce_fusion
  3.3 0.1 copy.15
  3.5 0.1 multiply_reduce_fusion.1
  3.6 0.1 copy.16
  3.6 0.7 reshape.56.info
  4.3 139.2 %shard_map.68 = (f32[4,128]{1,0:T(4,128)}, f32[4,128]{1,0:T(4,128)}, f32[32,512]{1,0:T(8,128)}) custom-call(s32[8,12]{1,0:T(8,128)} %reshape.56.info, bf16[512,1024]{1,0:T(8,128)(2,1)} %feats.1, s32[8,512]{1,0:T(8,128)} %bitcast.15, bf16[4,256,1024]{2,1,0:T(8,128)(2,1)} %rows.1), custom_call_target="tpu_custom_call" | custom-call | tf_op jit(solution)/shard_map/pallas_call | solution.py:691
  143.6 1.3 subtract_bitcast_fusion
  144.8 1.5 convert_bitcast_fusion
  (5 shorter events, 0.1 us)
Async XLA Ops:
  0.6 0.8 copy-start
